TPU v7x, 512 devices: a whole 4x8x8 slice. The times are simulated.
512 devices in a mesh: row: 128 (over y, z, core), samp: 4 (over x).
Axes of the slice: x: 4, y: 8, z: 8, core: 2. Of those that a mesh axis runs over, the one named last changes fastest.
Arguments:
- probe: bfloat16 [32768, 2, 512], P('row', None, 'samp'), may hold values from -6 to 6
- shift_real: float32 [32768], P('row'), may hold values from -3 to -0.5
- shift_imag: float32 [32768], P('row'), may hold values from 0.1 to 1
- child_gen: bfloat16 [65536, 128], P('row'), may hold values from -0.75 to 0.75
- child_coef: bfloat16 [2, 64, 512], P(None, None, 'samp'), may hold values from -6 to 6
- child_map: int32 [512, 128], P('row'), may hold values from -1 to 32767, as said below
- child_of: int32 [512], P('row'), may hold values from 0 to 1
- leaf_skel: int32 [128, 128], P('row'), may hold values from 0 to 511, as said below
- pair_skel: int32 [64, 128], replicated, may hold values from 0 to 255, as said below
- quad_skel: int32 [32, 128], replicated, may hold values from 0 to 255, as said below
Outputs:
- samples: float32 [32768, 2, 512], P('row', None, 'samp')
- leaf_interp: float32 [65536, 128], P('row')
- merge_interp: float32 [16384, 128], P('row')
- top_interp: float32 [8192, 128], P('row')
- top_samples: float32 [4096, 512], P('row', 'samp')
Inputs may be any that keep to these rules, and one draw needn't show every extreme that they name: `child_map`: entries are front rows or -1; -1 entries stand only at the end of a block. The rows of one index of row name at most 8 rows of one leaf (rows with equal g // 256), all different; some leaf receives exactly 8 rows from every index of row. `leaf_skel`: each row holds 128 different increasing row numbers of the leaf. `pair_skel`: each row holds 128 different increasing candidate numbers. `quad_skel`: each row holds 128 different increasing candidate numbers.
All inputs are finite; a program needn't handle non-finite values.
Results may differ from a plain program's by a relative error of at most 0.0015.
Values may be sent and summed in bfloat16 or wider, within the bound.
No kernel may reach another device: no remote copies, remote signals or barrier semaphores. Data moves between devices by JAX's collectives and lax.ppermute only.
A program may use at most 64 MiB of HBM per device.

v0:
```python
import jax
import jax.numpy as jnp
from jax import lax
from jax.sharding import PartitionSpec as P

LINE = 512


highest = lax.Precision.HIGHEST


def with_halo(x, sides, width):
    for axis, dim in sides:
        count, length = (lax.axis_size(axis), x.shape[dim])
        up = [(i, (i + 1) % count) for i in range(count - 1)]
        down = [(j, i) for i, j in up]
        last = lax.slice_in_dim(x, length - width, length, axis=dim)
        first = lax.slice_in_dim(x, 0, width, axis=dim)
        before = lax.ppermute(last, axis, up)
        after = lax.ppermute(first, axis, down)
        x = jnp.concatenate([before, x, after], axis=dim)
    return x


def shifted(value, axis, steps):
    count = lax.axis_size(axis)
    first, last = (max(0, -steps), min(count, count - steps))
    return lax.ppermute(value, axis, [(source, source + steps) for source in range(first, last)])


def swapped(block, axis, apart):
    count = lax.axis_size(axis)
    route = []
    for low in range(count):
        high = low | 1 << apart
        if high != low and high < count:
            route += [(low, high), (high, low)]
    return lax.ppermute(block, axis, route)


def products(targets, chosen):
    gram_matrix = jnp.dot(chosen, chosen.T, precision=highest, preferred_element_type=jnp.float32)
    cross_terms = jnp.dot(targets, chosen.T, precision=highest, preferred_element_type=jnp.float32)
    return (gram_matrix, cross_terms)


def solved(gram_matrix, cross_terms):
    factor = jnp.linalg.cholesky(gram_matrix)
    return jax.scipy.linalg.cho_solve((factor, True), cross_terms.T).T


def child_samples(generators, labels, child_coef):
    row_count = generators.shape[0]
    rank_width = child_coef.shape[1]
    stacked = generators.reshape(row_count * 2, rank_width)
    is_first = jnp.repeat(labels == 0, 2)[:, None]
    nothing = jnp.zeros_like(stacked)
    widened = jnp.concatenate(
        [jnp.where(is_first, stacked, nothing), jnp.where(is_first, nothing, stacked)], 1
    )
    coef_table = child_coef.reshape(2 * rank_width, child_coef.shape[2])
    product = jnp.dot(widened, coef_table, preferred_element_type=jnp.float32)
    return product.reshape(row_count, 2, child_coef.shape[2]).astype(jnp.bfloat16)


def sparse_part(probe, shift_real, shift_imag):
    row_count = probe.shape[0]
    rimmed = with_halo(probe, (("row", 0),), 1)
    offset = max(1, LINE // row_count)
    from_below = shifted(probe, "row", offset)
    from_above = shifted(probe, "row", -offset)
    centre = probe.astype(jnp.float32)
    left_side = rimmed[:-2].astype(jnp.float32)
    right_side = rimmed[2:].astype(jnp.float32)
    laplace = (
        4.0 * centre
        - left_side
        - right_side
        - from_below.astype(jnp.float32)
        - from_above.astype(jnp.float32)
    )
    turned = jnp.stack([-centre[:, 1], centre[:, 0]], 1)
    return laplace + shift_real[:, None, None] * centre + shift_imag[:, None, None] * turned


def body(
    probe,
    shift_real,
    shift_imag,
    child_gen,
    child_coef,
    child_map,
    child_of,
    leaf_skel,
    pair_skel,
    quad_skel,
):
    row_count = probe.shape[0]
    col_count = probe.shape[2]
    devices = lax.axis_size("row")
    position = lax.axis_index("row")
    front = sparse_part(probe, shift_real, shift_imag)
    targets = child_map.reshape(-1)
    labels = jnp.repeat(child_of, child_map.shape[1])
    capacity = 2 * targets.shape[0] // devices
    is_valid = targets >= 0
    owners = jnp.where(is_valid, targets // row_count, devices)
    matches = (owners[:, None] == jnp.arange(devices)[None, :]).astype(jnp.int32)
    earlier = jnp.cumsum(matches, 0) - matches
    within = jnp.sum(earlier * matches, 1)
    slot_index = jnp.where(is_valid, owners * capacity + within, devices * capacity)
    local_rows = jnp.where(is_valid, targets - owners * row_count, -1)
    places = (
        jnp.full((devices * capacity,), -1, jnp.int32).at[slot_index].set(local_rows, mode="drop")
    )
    values_out = child_samples(child_gen, labels, child_coef)
    outgoing = (
        jnp.zeros((devices * capacity, 2, col_count), jnp.bfloat16)
        .at[slot_index]
        .set(values_out, mode="drop")
    )
    arrived, got_places = (
        lax.all_to_all(outgoing, "row", split_axis=0, concat_axis=0, tiled=True),
        lax.all_to_all(places, "row", split_axis=0, concat_axis=0, tiled=True),
    )
    landing = jnp.where(got_places < 0, row_count, got_places)
    samples = front.at[landing].add(arrived.astype(jnp.float32), mode="drop")
    leaf_rows = samples.reshape(2 * row_count, col_count)
    chosen = leaf_rows[leaf_skel[0]]
    partner = swapped(chosen, "row", 0)
    low_bit = position % 2
    high_bit = position // 2 % 2
    pair_cand = jnp.where(
        low_bit == 0, jnp.concatenate([chosen, partner], 0), jnp.concatenate([partner, chosen], 0)
    )
    pair_picks = lax.dynamic_index_in_dim(pair_skel, position // 2, 0, keepdims=False)
    pair_chosen = pair_cand[pair_picks]
    sibling = swapped(pair_chosen, "row", 1)
    quad_cand = jnp.where(
        high_bit == 0,
        jnp.concatenate([pair_chosen, sibling], 0),
        jnp.concatenate([sibling, pair_chosen], 0),
    )
    quad_picks = lax.dynamic_index_in_dim(quad_skel, position // 4, 0, keepdims=False)
    quad_chosen = quad_cand[quad_picks]
    rank_width = chosen.shape[0]
    half_rank = rank_width // 2
    quarter_rank = rank_width // 4
    own_top = lax.dynamic_slice_in_dim(pair_chosen, low_bit * half_rank, half_rank, 0)
    terms = (
        products(leaf_rows, chosen) + products(chosen, pair_chosen) + products(own_top, quad_chosen)
    )
    terms = lax.psum(terms, "samp")
    leaf_interp = solved(terms[0], terms[1])
    merge_interp = solved(terms[2], terms[3])
    top_interp = solved(terms[4], terms[5])
    top_rows = lax.dynamic_slice_in_dim(quad_chosen, position % 4 * quarter_rank, quarter_rank, 0)
    return (samples, leaf_interp, merge_interp, top_interp, top_rows)


def solution(mesh):
    return jax.shard_map(
        body,
        mesh=mesh,
        in_specs=(
            P("row", None, "samp"),
            P("row"),
            P("row"),
            P("row", None),
            P(None, None, "samp"),
            P("row", None),
            P("row"),
            P("row", None),
            P(),
            P(),
        ),
        out_specs=(
            P("row", None, "samp"),
            P("row", None),
            P("row", None),
            P("row", None),
            P("row", "samp"),
        ),
        check_vma=False,
    )
```

profile of v0, /device:TPU:1, one launch (start us, length us, event | category | flops | bytes accessed | tf_op | source)
XLA Modules:
  0.0 307.2 jit_solution(4382473456205231579)
XLA Ops:
  7.2 1.3 collective-permute-start.3
  8.5 5.5 %collective-permute-start.2 = (bf16[256,2,128]{2,1,0:T(2,128)(2,1)}, bf16[256,2,128]{2,1,0:T(2,128)(2,1)S(1)}, u32[]{:S(2)}, u32[]{:S(2)}) collective-permute-start(bf16[256,2,128]{2,1,0:T(2,128)(2,1)} %param.11), channel_id=1, source_target_pairs={{0,8},{4,12},{8,16},{12,20},{16,24},{20,28},{24,32},{28,36},{32,40... | collective-permute-start | bytes 393224 | tf_op jit(solution)/shard_map/ppermute | solution.py:28
  14.7 8.0 %collective-permute-start.1 = (bf16[1,2,128]{2,1,0:T(2,128)(2,1)S(1)}, bf16[1,2,128]{2,1,0:T(2,128)(2,1)S(1)}, u32[]{:S(2)}, u32[]{:S(2)}) collective-permute-start(bf16[1,2,128]{2,1,0:T(2,128)(2,1)S(1)} %get-tuple-element.16), channel_id=1, source_target_pairs={{4,0},{8,4},{12,8},{16,12},{20,16},{24,20},{28,24},{32,28},{36,32}... | collective-permute-start | bytes 1544 | tf_op jit(solution)/shard_map/ppermute | solution.py:20
  22.7 1.9 collective-permute-start
  25.3 2.4 scatter_custom_fusion
  28.5 16.6 %all-to-all-start = ((s32[128,8,1]{1,2,0:T(1,128)}), s32[128,8,1]{1,2,0:T(1,128)S(1)}, u32[]{:S(2)}, u32[]{:S(2)}) async-start(s32[128,8,1]{1,2,0:T(1,128)} %bitcast.7), calls=%async_computation | async-start | bytes 131072 | tf_op jit(solution)/shard_map/all_to_all | solution.py:124
  48.3 1.1 broadcast_in_dim.57
  49.3 47.7 %scatter_fusion = bf16[1024,2,128]{2,1,0:T(2,128)(2,1)} fusion(bf16[1024,2,128]{2,1,0:T(2,128)(2,1)} %broadcast_in_dim.57, s32[512]{0:T(512)S(1)} %bitcast.132, bf16[512,2,128]{2,1,0:T(2,128)(2,1)S(1)} %copy.40), kind=kCustom, calls=%fused_computation.4 | custom fusion | bytes 788480 | tf_op jit(solution)/shard_map/scatter | solution.py:120
  97.1 13.2 %all-to-all-start.1 = ((bf16[1024,2,128]{2,1,0:T(2,128)(2,1)}), bf16[1024,2,128]{2,1,0:T(2,128)(2,1)S(1)}, u32[]{:S(2)}, u32[]{:S(2)}) async-start(bf16[1024,2,128]{2,1,0:T(2,128)(2,1)} %scatter_fusion), calls=%async_computation.1 | async-start | bytes 1048576 | tf_op jit(solution)/shard_map/all_to_all | solution.py:123
  113.3 1.9 fusion
  115.2 14.5 %all-to-all-done.1 = bf16[1024,2,128]{2,1,0:T(2,128)(2,1)S(1)} async-done(((bf16[1024,2,128]{2,1,0:T(2,128)(2,1)}), bf16[1024,2,128]{2,1,0:T(2,128)(2,1)S(1)}, u32[]{:S(2)}, u32[]{:S(2)}) %all-to-all-start.1) | async-done | bytes 524320 | tf_op jit(solution)/shard_map/all_to_all | solution.py:123
  130.1 35.3 %scatter_fusion.1 = f32[256,2,128]{2,1,0:T(2,128)S(1)} fusion(f32[256,2,128]{2,1,0:T(2,128)S(1)} %fusion, s32[1024]{0:T(1024)S(1)} %bitcast.129, f32[1024,2,128]{2,1,0:T(2,128)S(1)} %convert_element_type.36), kind=kCustom, calls=%fused_computation.5 | custom fusion | flops 262144 | bytes 3149824 | tf_op jit(solution)/shard_map/scatter-add | solution.py:127
  166.1 1.1 fusion.51
  167.2 1.9 collective-permute-start.4
  169.1 0.9 fusion.50
  171.0 0.9 fusion.53
  171.9 1.9 collective-permute-start.5
  173.8 0.9 fusion.52
  174.7 2.6 collective-permute-done.5
  178.0 0.9 fusion.54
  179.1 13.5 %psum.47 = f32[64,128]{1,0:T(8,128)S(1)} all-reduce(f32[64,128]{1,0:T(8,128)S(1)} %fusion.27), channel_id=1, replica_groups=mesh['row'=128,'samp'=4] {'samp'}, use_global_device_ids=true, to_apply=%region_13.15 | all-reduce | flops 8192 | bytes 65536 | tf_op jit(solution)/shard_map/psum | solution.py:153
  193.3 32.3 %all-reduce.3.cloned.1.call-done = (f32[512,128]{1,0:T(8,128)}, f32[128,128]{0,1:T(8,128)}, f32[128,128]{1,0:T(8,128)}, f32[128,128]{0,1:T(8,128)}, f32[128,128]{0,1:T(8,128)}) async-done(((f32[512,128]{1,0:T(8,128)}, f32[128,128]{0,1:T(8,128)}, f32[128,128]{1,0:T(8,128)}, f32[128,128]{0,1:T(8,128)}, f32[128,128]{0,1:T(8,128)}), (f32[512,128]{1,0:T(8,128)}, f32[128,128]{0,1:T(8,128)}, f32[128,128]{1,0:T(8,128)}, ...) | async-done | bytes 524304 | tf_op jit(solution)/shard_map/psum | solution.py:153
  225.6 1.0 copy.42
  226.6 11.7 %cholesky.59 = f32[128,128]{1,0:T(8,128)S(1)} custom-call(f32[128,128]{1,0:T(8,128)S(1)} %fusion.26), custom_call_target="Cholesky" | custom-call | tf_op jit(solution)/shard_map/jit(cholesky)/cholesky | solution.py:48
  239.6 9.8 %custom-call.23 = f32[1,128,128]{1,2,0:T(8,128)S(1)} custom-call(f32[1,128,128]{2,1,0:T(8,128)S(1)} %fusion.9), custom_call_target="InvertDiagBlocksLowerTriangular" | custom-call | tf_op jit(solution)/shard_map/jit(_cho_solve)/triangular_solve | solution.py:49
  249.9 1.3 fusion.22
  252.2 11.7 %cholesky.70 = f32[128,128]{1,0:T(8,128)S(1)} custom-call(f32[128,128]{1,0:T(8,128)S(1)} %get-tuple-element.18), custom_call_target="Cholesky" | custom-call | tf_op jit(solution)/shard_map/jit(cholesky)/cholesky | solution.py:48
  265.3 10.0 %custom-call.24 = f32[1,128,128]{1,2,0:T(8,128)S(1)} custom-call(f32[1,128,128]{2,1,0:T(8,128)S(1)} %fusion.10), custom_call_target="InvertDiagBlocksLowerTriangular" | custom-call | tf_op jit(solution)/shard_map/jit(_cho_solve)/triangular_solve | solution.py:49
  275.5 0.9 fusion.17
  276.5 11.7 %cholesky.81 = f32[128,128]{1,0:T(8,128)S(1)} custom-call(f32[128,128]{1,0:T(8,128)S(1)} %get-tuple-element.17), custom_call_target="Cholesky" | custom-call | tf_op jit(solution)/shard_map/jit(cholesky)/cholesky | solution.py:48
  289.5 9.8 %custom-call.25 = f32[1,128,128]{1,2,0:T(8,128)S(1)} custom-call(f32[1,128,128]{2,1,0:T(8,128)S(1)} %fusion.11), custom_call_target="InvertDiagBlocksLowerTriangular" | custom-call | tf_op jit(solution)/shard_map/jit(_cho_solve)/triangular_solve | solution.py:49
  299.5 0.9 fusion.12
  (94 shorter events, 17.6 us)
Async XLA Ops:
  7.2 39.6 %copy-start = (bf16[2,64,128]{2,1,0:T(8,128)(2,1)S(1)}, bf16[2,64,128]{2,1,0:T(8,128)(2,1)}, u32[]{:S(2)}) copy-start(bf16[2,64,128]{2,1,0:T(8,128)(2,1)} %param.15) | copy-start | bytes 98308
  7.2 105.5 %collective-permute-start.3 = (bf16[256,2,128]{2,1,0:T(2,128)(2,1)}, bf16[256,2,128]{2,1,0:T(2,128)(2,1)S(1)}, u32[]{:S(2)}, u32[]{:S(2)}) collective-permute-start(bf16[256,2,128]{2,1,0:T(2,128)(2,1)} %param.11), channel_id=1, source_target_pairs={{8,0},{12,4},{16,8},{20,12},{24,16},{28,20},{32,24},{36,28},{40,32... | collective-permute-start | bytes 393224 | tf_op jit(solution)/shard_map/ppermute | solution.py:28
  8.5 104.2 %collective-permute-start.2 = (bf16[256,2,128]{2,1,0:T(2,128)(2,1)}, bf16[256,2,128]{2,1,0:T(2,128)(2,1)S(1)}, u32[]{:S(2)}, u32[]{:S(2)}) collective-permute-start(bf16[256,2,128]{2,1,0:T(2,128)(2,1)} %param.11), channel_id=1, source_target_pairs={{0,8},{4,12},{8,16},{12,20},{16,24},{20,28},{24,32},{28,36},{32,40... | collective-permute-start | bytes 393224 | tf_op jit(solution)/shard_map/ppermute | solution.py:28
  14.7 9.9 %copy-start.9 = (s32[4,128]{1,0:T(4,128)S(1)}, s32[4,128]{1,0:T(4,128)}, u32[]{:S(2)}) copy-start(s32[4,128]{1,0:T(4,128)} %param.16) | copy-start | bytes 6148
  14.7 98.0 %collective-permute-start.1 = (bf16[1,2,128]{2,1,0:T(2,128)(2,1)S(1)}, bf16[1,2,128]{2,1,0:T(2,128)(2,1)S(1)}, u32[]{:S(2)}, u32[]{:S(2)}) collective-permute-start(bf16[1,2,128]{2,1,0:T(2,128)(2,1)S(1)} %get-tuple-element.16), channel_id=1, source_target_pairs={{4,0},{8,4},{12,8},{16,12},{20,16},{24,20},{28,24},{32,28},{36,32}... | collective-permute-start | bytes 1544 | tf_op jit(solution)/shard_map/ppermute | solution.py:20
  22.7 90.0 %collective-permute-start = (bf16[1,2,128]{2,1,0:T(2,128)(2,1)S(1)}, bf16[1,2,128]{2,1,0:T(2,128)(2,1)S(1)}, u32[]{:S(2)}, u32[]{:S(2)}) collective-permute-start(bf16[1,2,128]{2,1,0:T(2,128)(2,1)S(1)} %get-tuple-element.15), channel_id=1, source_target_pairs={{0,4},{4,8},{8,12},{12,16},{16,20},{20,24},{24,28},{28,32},{32,36}... | collective-permute-start | bytes 1544 | tf_op jit(solution)/shard_map/ppermute | solution.py:19
  25.3 19.8 %copy-start.7 = (bf16[512,128]{1,0:T(8,128)(2,1)S(1)}, bf16[512,128]{1,0:T(8,128)(2,1)}, u32[]{:S(2)}) copy-start(bf16[512,128]{1,0:T(8,128)(2,1)} %param.14) | copy-start | bytes 393220
  28.5 68.5 %all-to-all-start = ((s32[128,8,1]{1,2,0:T(1,128)}), s32[128,8,1]{1,2,0:T(1,128)S(1)}, u32[]{:S(2)}, u32[]{:S(2)}) async-start(s32[128,8,1]{1,2,0:T(1,128)} %bitcast.7), calls=%async_computation | async-start | bytes 131072 | tf_op jit(solution)/shard_map/all_to_all | solution.py:124
  45.2 0.7 copy-start.12
  45.9 0.7 copy-start.13
  46.7 1.0 copy-start.2
  97.1 32.7 %all-to-all-start.1 = ((bf16[1024,2,128]{2,1,0:T(2,128)(2,1)}), bf16[1024,2,128]{2,1,0:T(2,128)(2,1)S(1)}, u32[]{:S(2)}, u32[]{:S(2)}) async-start(bf16[1024,2,128]{2,1,0:T(2,128)(2,1)} %scatter_fusion), calls=%async_computation.1 | async-start | bytes 1048576 | tf_op jit(solution)/shard_map/all_to_all | solution.py:123
  110.3 115.3 %all-reduce.3.cloned.1.call-start = ((), (), s32[]{:S(2)}) async-start(), calls=%async_computation.2 | async-start | bytes 1048576 | tf_op jit(solution)/shard_map/psum | solution.py:153
  112.6 0.7 copy-start.10
  112.6 0.7 copy-start.11
  165.4 0.7 copy-start.1
  167.2 3.1 %collective-permute-start.4 = (f32[128,128]{1,0:T(8,128)S(1)}, f32[128,128]{1,0:T(8,128)S(1)}, u32[]{:S(2)}, u32[]{:S(2)}) collective-permute-start(f32[128,128]{1,0:T(8,128)S(1)} %gather_fusion), channel_id=1, source_target_pairs={{0,4},{4,0},{8,12},{12,8},{16,20},{20,16},{24,28},{28,24},{32,36},... | collective-permute-start | bytes 196616 | tf_op jit(solution)/shard_map/ppermute | solution.py:38
  171.9 5.4 %collective-permute-start.5 = (f32[128,128]{1,0:T(8,128)S(1)}, f32[128,128]{1,0:T(8,128)S(1)}, u32[]{:S(2)}, u32[]{:S(2)}) collective-permute-start(f32[128,128]{1,0:T(8,128)S(1)} %gather_fusion.1), channel_id=1, source_target_pairs={{0,8},{8,0},{4,12},{12,4},{16,24},{24,16},{20,28},{28,20},{32,40},... | collective-permute-start | bytes 196616 | tf_op jit(solution)/shard_map/ppermute | solution.py:38
  225.6 1.0 copy-start.3
  225.6 23.9 %copy-start.4 = (f32[512,128]{1,0:T(8,128)S(1)}, f32[512,128]{1,0:T(8,128)}, u32[]{:S(2)}) copy-start(f32[512,128]{1,0:T(8,128)} %get-tuple-element.6) | copy-start | bytes 786436
  249.9 1.3 copy-start.6
  251.2 0.8 copy-start.5
  264.6 10.7 %copy-start.8 = (f32[128,128]{1,0:T(8,128)S(1)}, f32[128,128]{1,0:T(8,128)}, u32[]{:S(2)}) copy-start(f32[128,128]{1,0:T(8,128)} %get-tuple-element.8) | copy-start | bytes 196612
Sparse Core Ops, SparseCore 0:
  179.0 46.5 all-reduce.2
where the time goes:
time: 309 us; the launch traced here: 307 us
  other arithmetic  110 us (36%)
  local copies, waits for them, and re-layouts  60.3 us (20%)
  starting transfers between devices  50.3 us (16%)
  waiting for transfers between devices  49.8 us (16%)
  between operations  14.7 us (5%)
  blocking collectives  13.5 us (4%)
  matrix products  9.11 us (3%)
    scatter x1, local copies, waits for them, and re-layouts, body(): outgoing = jnp.zeros((devices * capacity, 2, col_count), jnp.bfloat16).at...  47.7 us
    another operation x9, other arithmetic, solved(): factor = jnp.linalg.cholesky(gram_matrix)  37.2 us
    scatter-add x1, other arithmetic, body(): samples = front.at[landing].add(arrived.astype(jnp.float32), mode='drop')  35.3 us
    psum x1, waiting for transfers between devices, body(): terms = lax.psum(terms, 'samp')  32.3 us
    another operation x6, other arithmetic, solved(): return jax.scipy.linalg.cho_solve((factor, True), cross_terms.T).T  31.6 us
    all_to_all x1, starting transfers between devices, body(): lax.all_to_all(places, 'row', split_axis=0, concat_axis=0, tiled=True)  16.6 us
    all_to_all x1, waiting for transfers between devices, body(): lax.all_to_all(outgoing, 'row', split_axis=0, concat_axis=0, tiled=True)  14.5 us
    psum x1, blocking collectives, body(): terms = lax.psum(terms, 'samp')  13.5 us
  transfers between devices with their start and end apart: 9, of which 4 were waited for; matrix products, arithmetic and copies ran while one was open for 20% of the time, Pallas kernels for 0%

commit v1 on v0

v1 whole, which is shorter than its diff:
```python
import functools

import jax
import jax.numpy as jnp
from jax import lax
from jax.experimental import pallas as pl
from jax.experimental.pallas import tpu as pltpu
from jax.sharding import PartitionSpec as P

LINE = 512
CAP = 8
SLOT = CAP + 2
RANK = 128
ROWS = 256
HIGHEST = lax.Precision.HIGHEST
F32 = jnp.float32
BF16 = jnp.bfloat16
VMEM_LIMIT = 48 * 1024 * 1024


def iota(shape, dim):
    return lax.broadcasted_iota(jnp.int32, shape, dim)


def column_of(row):
    square = jnp.broadcast_to(row, (128, 128))
    return jnp.sum(jnp.where(iota((128, 128), 0) == iota((128, 128), 1), square, jnp.zeros_like(square)), 1, keepdims=True)


def side_by_side(ref):
    return jnp.concatenate([ref[s] for s in range(ref.shape[0])], 1)


def dot(a, b, dims=(((1,), (0,)), ((), ())), precision=None):
    return lax.dot_general(a, b, dims, precision=precision, preferred_element_type=F32)


ROW_ROW = (((1,), (1,)), ((), ()))
COL_COL = (((0,), (0,)), ((), ()))


def route_kernel(of_ref, map_ref, gen_ref, out_ref):
    blocks = map_ref.shape[0]
    count = blocks * 128
    targets = map_ref[...]
    owner = lax.shift_right_arithmetic(targets, 8)
    place = (targets & (ROWS - 1)) + 1
    owner_row = jnp.concatenate([owner[b : b + 1] for b in range(blocks)], 1).astype(F32)
    owner_col = jnp.concatenate([column_of(owner[b : b + 1].astype(F32)) for b in range(blocks)], 0)
    place_col = jnp.concatenate([column_of(place[b : b + 1].astype(F32)) for b in range(blocks)], 0)
    label_col = jnp.concatenate([jnp.full((128, 1), of_ref[b], jnp.int32) for b in range(blocks)], 0).astype(F32)
    same = jnp.where(owner_col == owner_row, 1.0, 0.0)
    sub, lane = iota((count, count), 0), iota((count, count), 1)
    within_row = jnp.sum(jnp.where(sub < lane, same, 0.0), 0, keepdims=True)
    within_col = jnp.sum(jnp.where(lane < sub, same, 0.0), 1, keepdims=True)
    slot_row = jnp.where(owner_row >= 0, owner_row * SLOT + within_row, -1.0).astype(jnp.int32)
    info_row = jnp.where(owner_row >= 0, owner_row * SLOT + CAP, -1.0).astype(jnp.int32)
    lanes = iota((count, 128), 1)
    within_at = within_col.astype(jnp.int32)
    info = jnp.where(lanes == within_at, place_col, 0.0) + jnp.where(lanes == within_at + CAP, label_col, 0.0)
    table = jnp.concatenate([gen_ref[...], info.astype(BF16)], 0)
    rows = out_ref.shape[0]
    step = min(256, rows)
    for first in range(0, rows, step):
        at = iota((step, count), 0) + first
        pick = jnp.concatenate([jnp.where(at == slot_row, 1.0, 0.0), jnp.where(at == info_row, 1.0, 0.0)], 1)
        out_ref[first : first + step] = dot(pick.astype(BF16), table).astype(BF16)


def route(child_map, child_of, child_gen, devices):
    return pl.pallas_call(
        route_kernel,
        out_shape=jax.ShapeDtypeStruct((devices * SLOT, child_gen.shape[1]), BF16),
        in_specs=[pl.BlockSpec(memory_space=pltpu.SMEM)] + [pl.BlockSpec(memory_space=pltpu.VMEM)] * 2,
        out_specs=pl.BlockSpec(memory_space=pltpu.VMEM),
        compiler_params=pltpu.CompilerParams(vmem_limit_bytes=VMEM_LIMIT),
        name="route",
    )(child_of, child_map, child_gen)


def front_kernel(x_ref, low_ref, high_ref, left_ref, right_ref, real_ref, imag_ref, coef_ref, out_ref):
    x = x_ref[...].astype(F32)
    rows = x.shape[0]
    sub = iota(x.shape, 0)
    left, right = left_ref[...].astype(F32), right_ref[...].astype(F32)
    before = jnp.where(sub == 0, left[0:1], jnp.where(sub == 1, left[1:2], pltpu.roll(x, 2, 0)))
    after = jnp.where(
        sub == rows - 2, right[0:1], jnp.where(sub == rows - 1, right[1:2], pltpu.roll(x, rows - 2, 0))
    )
    turned = jnp.where((sub & 1) == 0, -pltpu.roll(x, rows - 1, 0), pltpu.roll(x, 1, 0))
    half = lax.shift_right_arithmetic(iota((256, 128), 0), 1) == iota((256, 128), 1)

    def spread(ref):
        blocks = [jnp.sum(jnp.where(half, ref[b : b + 1, :], 0.0), 1, keepdims=True) for b in range(ref.shape[0])]
        return jnp.concatenate(blocks, 0)

    laplace = 4.0 * x - before - after - low_ref[...].astype(F32) - high_ref[...].astype(F32)
    out_ref[0:rows] = laplace + spread(real_ref) * x + spread(imag_ref) * turned
    out_ref[rows:] = coef_ref[...].astype(F32)


def front(x, low, high, left, right, real, imag, coef):
    return pl.pallas_call(
        front_kernel,
        out_shape=jax.ShapeDtypeStruct((x.shape[0] + coef.shape[0], x.shape[1]), F32),
        in_specs=[pl.BlockSpec(memory_space=pltpu.VMEM)] * 8,
        out_specs=pl.BlockSpec(memory_space=pltpu.VMEM),
        compiler_params=pltpu.CompilerParams(vmem_limit_bytes=VMEM_LIMIT),
        name="front",
    )(x, low, high, left, right, real, imag, coef)


def leaf_kernel(where_ref, got_ref, wide_ref, skel_ref, own_ref, leaf_ref, chosen_ref):
    rows = 2 * ROWS
    got = got_ref[...]
    count = got.shape[0]
    sources = count // SLOT
    info_at = iota((sources, count), 0) * SLOT + CAP == iota((sources, count), 1)
    info = dot(jnp.where(info_at, 1.0, 0.0).astype(BF16), got).astype(BF16)
    along = iota((count, sources), 0)
    source = lax.shift_right_arithmetic(along * 6554, 16)
    spread = dot(jnp.where(source == iota((count, sources), 1), 1.0, 0.0).astype(BF16), info)
    sub = iota((count, 128), 0)
    slot = sub - SLOT * lax.shift_right_arithmetic(sub * 6554, 16)
    label = jnp.sum(jnp.where(iota((count, 128), 1) == slot + CAP, spread, 0.0), 1, keepdims=True)
    along_t = iota((sources, count), 1)
    source_t = lax.shift_right_arithmetic(along_t * 6554, 16)
    spread_t = dot(info, jnp.where(source_t == iota((sources, count), 0), 1.0, 0.0).astype(BF16), COL_COL)
    lane = iota((128, count), 1)
    slot_t = lane - SLOT * lax.shift_right_arithmetic(lane * 6554, 16)
    sub_t = iota((128, count), 0)
    code = jnp.sum(jnp.where((sub_t == slot_t) & (sub_t < CAP), spread_t, 0.0), 0, keepdims=True)
    onto = jnp.where(iota((ROWS, count), 0) + 1 == code.astype(jnp.int32), 1.0, 0.0).astype(BF16)
    wide = got.astype(F32)
    zero = jnp.zeros_like(wide)
    parts = jnp.concatenate([jnp.where(label == 0.0, wide, zero), jnp.where(label == 0.0, zero, wide)], 1).astype(BF16)
    rank = 64
    for s in range(wide_ref.shape[0]):
        coef = wide_ref[s, rows:, :].astype(BF16)
        first, second, none = coef[:rank], coef[rank:], jnp.zeros((rank, 128), BF16)
        table = jnp.concatenate(
            [jnp.concatenate([first, none, second, none], 0), jnp.concatenate([none, first, none, second], 0)], 1
        )
        values = dot(parts, table).astype(BF16)
        sums = dot(onto, values)
        for c in range(2):
            at = pl.ds(c, ROWS, stride=2)
            leaf_ref[s, at, :] = wide_ref[s, at, :] + sums[:, c * 128 : (c + 1) * 128]
    own_ref[...] = leaf_ref[where_ref[1]]
    picks = column_of(skel_ref[...].astype(F32)).astype(jnp.int32)
    chosen_ref[...] = dot(
        jnp.where(iota((RANK, rows), 1) == picks, 1.0, 0.0), side_by_side(leaf_ref), precision=HIGHEST
    )


def leaf(where, got, wide, skel):
    width = wide.shape[0] * wide.shape[2]
    return pl.pallas_call(
        leaf_kernel,
        out_shape=[
            jax.ShapeDtypeStruct((2 * ROWS, wide.shape[2]), F32),
            jax.ShapeDtypeStruct((wide.shape[0], 2 * ROWS, wide.shape[2]), F32),
            jax.ShapeDtypeStruct((RANK, width), F32),
        ],
        in_specs=[pl.BlockSpec(memory_space=pltpu.SMEM)] + [pl.BlockSpec(memory_space=pltpu.VMEM)] * 3,
        out_specs=[pl.BlockSpec(memory_space=pltpu.VMEM)] * 3,
        compiler_params=pltpu.CompilerParams(vmem_limit_bytes=VMEM_LIMIT),
        name="leaf",
    )(where, got, wide, skel)


def picked(skel_ref, group, low, own, other):
    picks = column_of(skel_ref[pl.ds(group, 1), :].astype(F32)).astype(jnp.int32)
    lane = iota((RANK, RANK), 1)
    onto_own = jnp.where(lane + RANK * low == picks, 1.0, 0.0)
    onto_other = jnp.where(lane + RANK * (1 - low) == picks, 1.0, 0.0)
    return dot(jnp.concatenate([onto_own, onto_other], 1), jnp.concatenate([own, other], 0), precision=HIGHEST)


def pair_kernel(where_ref, own_ref, other_ref, skel_ref, out_ref):
    position = where_ref[0]
    group, low = lax.shift_right_arithmetic(position, 1), position & 1
    out_ref[...] = picked(skel_ref, group, low, own_ref[...], other_ref[...])


def pair(where, own, other, skel):
    return pl.pallas_call(
        pair_kernel,
        out_shape=jax.ShapeDtypeStruct(own.shape, F32),
        in_specs=[pl.BlockSpec(memory_space=pltpu.SMEM)] + [pl.BlockSpec(memory_space=pltpu.VMEM)] * 3,
        out_specs=pl.BlockSpec(memory_space=pltpu.VMEM),
        compiler_params=pltpu.CompilerParams(vmem_limit_bytes=VMEM_LIMIT),
        name="pair",
    )(where, own, other, skel)


def invert_in_place(refs):
    sub = iota((8, 128), 0)
    lane = iota((8, 128), 1)

    def along(block, index):
        return jnp.take_along_axis(block, index, axis=1)

    def step(b, carry):
        base = pl.multiple_of(b * 8, 8)
        rows = pl.ds(base, 8)
        inside = (lane >= base) & (lane < base + 8)
        indices = [jnp.full((8, 128), base + k, jnp.int32) for k in range(8)]
        for ref in refs:
            block = ref[rows, :]
            columns = [along(block, indices[k]) for k in range(8)]
            block = jnp.where(inside, jnp.where(lane - base == sub, 1.0, 0.0), block)
            for i in range(8):
                pivot = columns[i][i : i + 1, :]
                scale = 1.0 / pivot
                minus = jnp.where(sub == i, columns[i] - 1.0, columns[i])
                block = block - minus * (block[i : i + 1, :] * scale)
                for k in range(i + 1, 8):
                    columns[k] = columns[k] - minus * (columns[k][i : i + 1, :] * scale)
            for m in range(16):
                part = ref[8 * m : 8 * m + 8, :]
                total = jnp.where(inside, 0.0, part)
                for k in range(8):
                    total = total - along(part, indices[k]) * block[k : k + 1, :]
                ref[8 * m : 8 * m + 8, :] = total
            ref[rows, :] = block
        return carry

    lax.fori_loop(0, 16, step, 0)


def interp_kernel(leaf_ref, chosen_ref, pair_ref, leaf_out, merge_out, first, second):
    chosen, upper = chosen_ref[...], pair_ref[...]
    first[...] = dot(chosen, chosen, ROW_ROW, HIGHEST)
    second[...] = dot(upper, upper, ROW_ROW, HIGHEST)
    invert_in_place([first, second])
    leaf_out[...] = dot(dot(side_by_side(leaf_ref), chosen, ROW_ROW, HIGHEST), first[...], precision=HIGHEST)
    merge_out[...] = dot(dot(chosen, upper, ROW_ROW, HIGHEST), second[...], precision=HIGHEST)


def interp(leaf_rows, chosen, upper):
    return pl.pallas_call(
        interp_kernel,
        out_shape=[
            jax.ShapeDtypeStruct((leaf_rows.shape[1], RANK), F32),
            jax.ShapeDtypeStruct((RANK, RANK), F32),
        ],
        in_specs=[pl.BlockSpec(memory_space=pltpu.VMEM)] * 3,
        out_specs=[pl.BlockSpec(memory_space=pltpu.VMEM)] * 2,
        scratch_shapes=[pltpu.VMEM((RANK, RANK), F32)] * 2,
        cost_estimate=pl.CostEstimate(flops=8_000_000_000, bytes_accessed=2_000_000, transcendentals=0),
        compiler_params=pltpu.CompilerParams(vmem_limit_bytes=VMEM_LIMIT),
        name="interp",
    )(leaf_rows, chosen, upper)


def top_kernel(where_ref, own_ref, other_ref, skel_ref, top_out, rows_out, gram, quad):
    position = where_ref[0]
    group, low, high = lax.shift_right_arithmetic(position, 2), position & 1, lax.shift_right_arithmetic(position, 1) & 1
    quad[...] = picked(skel_ref, group, high, own_ref[...], other_ref[...])
    chosen = quad[...]
    gram[...] = dot(chosen, chosen, ROW_ROW, HIGHEST)
    columns = pl.ds(pl.multiple_of(where_ref[1] * 128, 128), 128)
    rows_out[...] = quad[pl.ds(pl.multiple_of((position & 3) * (RANK // 4), RANK // 4), RANK // 4), columns]
    invert_in_place([gram])
    own = own_ref[pl.ds(pl.multiple_of(low * (RANK // 2), RANK // 2), RANK // 2), :]
    top_out[...] = dot(dot(own, chosen, ROW_ROW, HIGHEST), gram[...], precision=HIGHEST)


def top(where, own, other, skel):
    return pl.pallas_call(
        top_kernel,
        out_shape=[jax.ShapeDtypeStruct((RANK // 2, RANK), F32), jax.ShapeDtypeStruct((RANK // 4, 128), F32)],
        in_specs=[pl.BlockSpec(memory_space=pltpu.SMEM)] + [pl.BlockSpec(memory_space=pltpu.VMEM)] * 3,
        out_specs=[pl.BlockSpec(memory_space=pltpu.VMEM)] * 2,
        scratch_shapes=[pltpu.VMEM((RANK, RANK), F32), pltpu.VMEM(own.shape, F32)],
        compiler_params=pltpu.CompilerParams(vmem_limit_bytes=VMEM_LIMIT),
        name="top",
    )(where, own, other, skel)


def shifted(value, axis, steps):
    count = lax.axis_size(axis)
    first, last = (max(0, -steps), min(count, count - steps))
    return lax.ppermute(value, axis, [(source, source + steps) for source in range(first, last)])


def swapped(block, axis, apart):
    count = lax.axis_size(axis)
    return lax.ppermute(block, axis, [(i, i ^ (1 << apart)) for i in range(count)])


def body(
    probe, shift_real, shift_imag, child_gen, child_coef, child_map, child_of, leaf_skel, pair_skel, quad_skel
):
    row_count, _, col_count = probe.shape
    devices = lax.axis_size("row")
    where = jnp.stack([lax.axis_index("row"), lax.axis_index("samp")]).astype(jnp.int32)
    offset = LINE // row_count
    low = shifted(probe, "row", offset)
    high = shifted(probe, "row", -offset)
    left = shifted(probe[row_count - 1 :], "row", 1)
    right = shifted(probe[:1], "row", -1)
    outgoing = route(child_map, child_of, child_gen, devices)
    flat = lambda value: value.reshape(-1, col_count)
    part = front(
        flat(probe), flat(low), flat(high), flat(left), flat(right),
        shift_real.reshape(-1, 128), shift_imag.reshape(-1, 128), flat(child_coef),
    )
    wide = lax.all_gather(part, "samp")
    got = lax.all_to_all(
        outgoing.reshape(devices * SLOT // 2, 2, -1), "row", split_axis=0, concat_axis=0, tiled=True
    ).reshape(devices * SLOT, -1)
    own, leaf_rows, chosen = leaf(where, got, wide, leaf_skel)
    upper = pair(where, chosen, swapped(chosen, "row", 0), pair_skel)
    across = swapped(upper, "row", 1)
    leaf_interp, merge_interp = interp(leaf_rows, chosen, upper)
    top_interp, top_rows = top(where, upper, across, quad_skel)
    return own.reshape(row_count, 2, col_count), leaf_interp, merge_interp, top_interp, top_rows


def solution(mesh):
    return jax.shard_map(
        body,
        mesh=mesh,
        in_specs=(
            P("row", None, "samp"),
            P("row"),
            P("row"),
            P("row", None),
            P(None, None, "samp"),
            P("row", None),
            P("row"),
            P("row", None),
            P(),
            P(),
        ),
        out_specs=(
            P("row", None, "samp"),
            P("row", None),
            P("row", None),
            P("row", None),
            P("row", "samp"),
        ),
        check_vma=False,
    )
```

time: 309 us -> 113 us (0.37)
  other arithmetic: 110 us -> 0.08 us
  local copies, waits for them, and re-layouts: 60.3 us -> 7.27 us
  Pallas kernels: 0 us -> 35.1 us
  waiting for transfers between devices: 49.8 us -> 17.3 us
  blocking collectives: 13.5 us -> 0 us
  starting transfers between devices: 50.3 us -> 39 us
  matrix products: 9.11 us -> 0 us
    another operation x18 -> x1, other arithmetic: 69 us -> 0.08 us  [body(): jnp.stack([lax.axis_index('row'), lax.axis_index('samp')]).astype(jnp.int32)]
    scatter x2 -> x0, local copies, waits for them, and re-layouts: 50.1 us -> none  [the longest x1 47.7 us: body(): outgoing = jnp.zeros((devices * capacity, 2, col_count), jnp.bfloat16).at...]
    scatter-add x1 -> x0, other arithmetic: 35.3 us -> none  [body(): samples = front.at[landing].add(arrived.astype(jnp.float32), mode='drop')]
    pallas_call x0 -> x6, Pallas kernels: none -> 35.1 us  [the longest x1 16.8 us: interp(): pl.pallas_call(interp_kernel, out_shape=[jax.ShapeDtypeStruct((leaf_rows....]
    psum x1 -> x0, waiting for transfers between devices: 32.3 us -> none  [body(): terms = lax.psum(terms, 'samp')]
    psum x1 -> x0, blocking collectives: 13.5 us -> none  [body(): terms = lax.psum(terms, 'samp')]
    all_to_all x2 -> x1, starting transfers between devices: 29.8 us -> 17.4 us  [body(): lax.all_to_all(outgoing.reshape(devices * SLOT // 2, 2, -1), 'row', split...]
    ppermute x2 -> x4, starting transfers between devices: 6.76 us -> 15.6 us  [shifted(): lax.ppermute(value, axis, [(source, source + steps) for source in range(f...]
  transfers between devices with their start and end apart: 9 -> 8, of which waited for: 4 -> 3; matrix products, arithmetic and copies ran while one was open for 20% -> 1% of each run, Pallas kernels for 0% -> 17%
where the time goes in v1:
time: 113 us
  starting transfers between devices  39 us (35%)
  Pallas kernels  35.1 us (31%)
  waiting for transfers between devices  17.3 us (15%)
  between operations  14.1 us (12%)
  local copies, waits for them, and re-layouts  7.27 us (6%)
    all_to_all x1, starting transfers between devices, body(): lax.all_to_all(outgoing.reshape(devices * SLOT // 2, 2, -1), 'row', split...  17.4 us
    pallas_call x1, Pallas kernels, interp(): pl.pallas_call(interp_kernel, out_shape=[jax.ShapeDtypeStruct((leaf_rows....  16.8 us
    ppermute x4, starting transfers between devices, shifted(): lax.ppermute(value, axis, [(source, source + steps) for source in range(f...  15.6 us
    all_to_all x1, waiting for transfers between devices, body(): lax.all_to_all(outgoing.reshape(devices * SLOT // 2, 2, -1), 'row', split...  15.5 us
    pallas_call x1, Pallas kernels, top(): pl.pallas_call(top_kernel, out_shape=[jax.ShapeDtypeStruct((RANK // 2, RA...  9.92 us
    unnamed x22, local copies, waits for them, and re-layouts  6.59 us
    ppermute x2, starting transfers between devices, swapped(): lax.ppermute(block, axis, [(i, i ^ 1 << apart) for i in range(count)])  5.95 us
    pallas_call x1, Pallas kernels, leaf(): pl.pallas_call(leaf_kernel, out_shape=[jax.ShapeDtypeStruct((2 * ROWS, wi...  3.6 us
  transfers between devices with their start and end apart: 8, of which 3 were waited for; matrix products, arithmetic and copies ran while one was open for 1% of the time, Pallas kernels for 17%

profile of v1, /device:TPU:1, one launch (start us, length us, event | category | flops | bytes accessed | tf_op | source)
XLA Modules:
  0.0 112.9 jit_solution(5375099117671098950)
XLA Ops:
  7.2 0.0 all-gather.3.cloned.1.call-start
  7.2 4.8 %collective-permute-start = (bf16[256,2,128]{2,1,0:T(2,128)(2,1)}, bf16[256,2,128]{2,1,0:T(2,128)(2,1)S(1)}, u32[]{:S(2)}, u32[]{:S(2)}) collective-permute-start(bf16[256,2,128]{2,1,0:T(2,128)(2,1)} %param.10), channel_id=1, source_target_pairs={{0,8},{4,12},{8,16},{12,20},{16,24},{20,28},{24,32},{28,36},{32,40... | collective-permute-start | bytes 393224 | tf_op jit(solution)/shard_map/ppermute | solution.py:285
  12.1 1.3 %collective-permute-start.1 = (bf16[256,2,128]{2,1,0:T(2,128)(2,1)}, bf16[256,2,128]{2,1,0:T(2,128)(2,1)S(1)}, u32[]{:S(2)}, u32[]{:S(2)}) collective-permute-start(bf16[256,2,128]{2,1,0:T(2,128)(2,1)} %param.10), channel_id=1, source_target_pairs={{8,0},{12,4},{16,8},{20,12},{24,16},{28,20},{32,24},{36,28},{40,32... | collective-permute-start | bytes 393224 | tf_op jit(solution)/shard_map/ppermute | solution.py:285
  13.4 0.7 fusion
  14.0 5.2 %collective-permute-start.3 = (bf16[1,2,128]{2,1,0:T(2,128)(2,1)S(1)}, bf16[1,2,128]{2,1,0:T(2,128)(2,1)S(1)}, u32[]{:S(2)}, u32[]{:S(2)}) collective-permute-start(bf16[1,2,128]{2,1,0:T(2,128)(2,1)S(1)} %get-tuple-element.19), channel_id=1, source_target_pairs={{4,0},{8,4},{12,8},{16,12},{20,16},{24,20},{28,24},{32,28},{36,32}... | collective-permute-start | bytes 1544 | tf_op jit(solution)/shard_map/ppermute | solution.py:285
  19.3 4.2 %collective-permute-start.2 = (bf16[1,2,128]{2,1,0:T(2,128)(2,1)S(1)}, bf16[1,2,128]{2,1,0:T(2,128)(2,1)S(1)}, u32[]{:S(2)}, u32[]{:S(2)}) collective-permute-start(bf16[1,2,128]{2,1,0:T(2,128)(2,1)S(1)} %get-tuple-element.20), channel_id=1, source_target_pairs={{0,4},{4,8},{8,12},{12,16},{16,20},{20,24},{24,28},{28,32},{32,36}... | collective-permute-start | bytes 1544 | tf_op jit(solution)/shard_map/ppermute | solution.py:285
  23.5 0.0 collective-permute-done.3
  23.5 0.7 collective-permute-done.2
  24.2 0.0 collective-permute-done
  24.2 0.9 copy-done.1
  25.1 0.8 copy-done.3
  25.9 0.7 copy-done.7
  26.6 0.7 copy-done.8
  27.2 1.1 %front.1 = f32[640,128]{1,0:T(8,128)} custom-call(bf16[512,128]{1,0:T(8,128)(2,1)S(1)} %bitcast.16, bf16[512,128]{1,0:T(8,128)(2,1)S(1)} %bitcast.17, bf16[512,128]{1,0:T(8,128)(2,1)S(1)} %bitcast.18, bf16[2,128]{1,0:T(2,128)(2,1)S(1)} %bitcast.23, bf16[2,128]{1,0:T(2,128)(2,1)S(1)} %bitcast.22, f32[2,128]{1,0:T(2,128)S(1)} %bitcast.20, ...), custom_call_target="tpu_custom_call" | custom-call | tf_op jit(solution)/shard_map/front/pallas_call | solution.py:103
  28.4 0.0 all-gather.3.cloned.1.call-update
  28.4 0.0 copy-start.2
  28.4 0.9 copy-done.2
  29.3 0.7 copy-done.6
  30.0 0.7 copy-done.10
  30.6 2.6 %route.1 = bf16[1280,128]{1,0:T(8,128)(2,1)} custom-call(s32[4]{0:T(128)S(1)} %copy-done.10, s32[4,128]{1,0:T(4,128)S(1)} %copy-done.6, bf16[512,128]{1,0:T(8,128)(2,1)S(1)} %copy-done.2), custom_call_target="tpu_custom_call" | custom-call | tf_op jit(solution)/shard_map/route/pallas_call | solution.py:71
  33.3 17.4 %all-to-all-start = ((bf16[640,2,128]{2,1,0:T(2,128)(2,1)}), bf16[640,2,128]{2,1,0:T(2,128)(2,1)S(1)}, u32[]{:S(2)}, u32[]{:S(2)}) async-start(bf16[640,2,128]{2,1,0:T(2,128)(2,1)} %bitcast.2), calls=%async_computation | async-start | bytes 655360 | tf_op jit(solution)/shard_map/all_to_all | solution.py:311
  50.7 0.1 pad_add_fusion.where_ref
  50.8 15.5 %all-to-all-done = bf16[640,2,128]{2,1,0:T(2,128)(2,1)S(1)} async-done(((bf16[640,2,128]{2,1,0:T(2,128)(2,1)}), bf16[640,2,128]{2,1,0:T(2,128)(2,1)S(1)}, u32[]{:S(2)}, u32[]{:S(2)}) %all-to-all-start) | async-done | bytes 327712 | tf_op jit(solution)/shard_map/all_to_all | solution.py:311
  66.2 1.3 %copy-done = f32[2560,128]{1,0:T(8,128)S(1)} copy-done((f32[2560,128]{1,0:T(8,128)S(1)}, f32[2560,128]{1,0:T(8,128)}, u32[]{:S(2)}) %copy-start) | copy-done | bytes 1310744
  67.6 3.6 %leaf.1 = (f32[512,128]{1,0:T(8,128)}, f32[4,512,128]{2,1,0:T(8,128)S(1)}, f32[128,512]{1,0:T(8,128)S(1)}) custom-call(s32[2]{0:T(128)S(1)} %pad_add_fusion.where_ref, bf16[1280,128]{1,0:T(8,128)(2,1)S(1)} %bitcast.15, f32[4,640,128]{2,1,0:T(8,128)S(1)} %bitcast.14, s32[1,128]{1,0:T(1,128)S(1)} %copy-done.9), custom_call_target="tpu_custom_call" | custom-call | tf_op jit(solution)/shard_map/leaf/pallas_call | solution.py:158
  71.2 3.8 %collective-permute-start.4 = (f32[128,512]{1,0:T(8,128)S(1)}, f32[128,512]{1,0:T(8,128)S(1)}, u32[]{:S(2)}, u32[]{:S(2)}) collective-permute-start(f32[128,512]{1,0:T(8,128)S(1)} %get-tuple-element.14.own_ref.chosen_ref), channel_id=1, source_target_pairs={{0,4},{4,0},{8,12},{12,8},{16,20},{20,16},{24,28},{28,24},{32,36},... | collective-permute-start | bytes 786440 | tf_op jit(solution)/shard_map/ppermute | solution.py:290
  74.9 1.1 %collective-permute-done.4.other_ref = f32[128,512]{1,0:T(8,128)S(1)} collective-permute-done((f32[128,512]{1,0:T(8,128)S(1)}, f32[128,512]{1,0:T(8,128)S(1)}, u32[]{:S(2)}, u32[]{:S(2)}) %collective-permute-start.4) | collective-permute-done | bytes 262176 | tf_op jit(solution)/shard_map/ppermute | solution.py:290
  76.1 1.0 pair.1.pair_ref.own_ref
  77.1 2.2 %collective-permute-start.5 = (f32[128,512]{1,0:T(8,128)S(1)}, f32[128,512]{1,0:T(8,128)S(1)}, u32[]{:S(2)}, u32[]{:S(2)}) collective-permute-start(f32[128,512]{1,0:T(8,128)S(1)} %pair.1.pair_ref.own_ref), channel_id=1, source_target_pairs={{0,8},{4,12},{8,0},{12,4},{16,24},{20,28},{24,16},{28,20},{32,40},... | collective-permute-start | bytes 786440 | tf_op jit(solution)/shard_map/ppermute | solution.py:290
  79.3 0.0 copy-start.5
  79.3 16.8 %interp.1 = (f32[512,128]{1,0:T(8,128)}, f32[128,128]{1,0:T(8,128)}) custom-call(f32[4,512,128]{2,1,0:T(8,128)S(1)} %get-tuple-element.13.leaf_ref, f32[128,512]{1,0:T(8,128)S(1)} %get-tuple-element.14.own_ref.chosen_ref, f32[128,512]{1,0:T(8,128)S(1)} %pair.1.pair_ref.own_ref), custom_call_target="tpu_custom_call" | custom-call | flops 8000000000 | bytes 2000000 | tf_op jit(solution)/shard_map/interp/pallas_call | solution.py:242
  96.1 9.9 %top.1 = (f32[64,128]{1,0:T(8,128)}, f32[32,128]{1,0:T(8,128)}) custom-call(s32[2]{0:T(128)S(1)} %pad_add_fusion.where_ref, f32[128,512]{1,0:T(8,128)S(1)} %pair.1.pair_ref.own_ref, f32[128,512]{1,0:T(8,128)S(1)} %collective-permute-done.5.other_ref, s32[32,128]{1,0:T(8,128)S(1)} %copy-done.5), custom_call_target="tpu_custom_call" | custom-call | tf_op jit(solution)/shard_map/top/pallas_call | solution.py:271
  (15 shorter events, 0.0 us)
Async XLA Ops:
  7.2 59.1 %copy-start.9 = (s32[1,128]{1,0:T(1,128)S(1)}, s32[1,128]{1,0:T(1,128)}, u32[]{:S(2)}) copy-start(s32[1,128]{1,0:T(1,128)} %skel_ref.3) | copy-start | bytes 1540
  7.2 59.1 %all-gather.3.cloned.1.call-start = ((), (), s32[]{:S(2)}) async-start(), calls=%async_computation.1 | async-start | bytes 1638400 | tf_op jit(solution)/shard_map/all_gather | solution.py:310
  7.2 17.0 %collective-permute-start = (bf16[256,2,128]{2,1,0:T(2,128)(2,1)}, bf16[256,2,128]{2,1,0:T(2,128)(2,1)S(1)}, u32[]{:S(2)}, u32[]{:S(2)}) collective-permute-start(bf16[256,2,128]{2,1,0:T(2,128)(2,1)} %param.10), channel_id=1, source_target_pairs={{0,8},{4,12},{8,16},{12,20},{16,24},{20,28},{24,32},{28,36},{32,40... | collective-permute-start | bytes 393224 | tf_op jit(solution)/shard_map/ppermute | solution.py:285
  12.1 12.1 %collective-permute-start.1 = (bf16[256,2,128]{2,1,0:T(2,128)(2,1)}, bf16[256,2,128]{2,1,0:T(2,128)(2,1)S(1)}, u32[]{:S(2)}, u32[]{:S(2)}) collective-permute-start(bf16[256,2,128]{2,1,0:T(2,128)(2,1)} %param.10), channel_id=1, source_target_pairs={{8,0},{12,4},{16,8},{20,12},{24,16},{28,20},{32,24},{36,28},{40,32... | collective-permute-start | bytes 393224 | tf_op jit(solution)/shard_map/ppermute | solution.py:285
  14.0 9.5 %collective-permute-start.3 = (bf16[1,2,128]{2,1,0:T(2,128)(2,1)S(1)}, bf16[1,2,128]{2,1,0:T(2,128)(2,1)S(1)}, u32[]{:S(2)}, u32[]{:S(2)}) collective-permute-start(bf16[1,2,128]{2,1,0:T(2,128)(2,1)S(1)} %get-tuple-element.19), channel_id=1, source_target_pairs={{4,0},{8,4},{12,8},{16,12},{20,16},{24,20},{28,24},{32,28},{36,32}... | collective-permute-start | bytes 1544 | tf_op jit(solution)/shard_map/ppermute | solution.py:285
  19.3 4.9 %collective-permute-start.2 = (bf16[1,2,128]{2,1,0:T(2,128)(2,1)S(1)}, bf16[1,2,128]{2,1,0:T(2,128)(2,1)S(1)}, u32[]{:S(2)}, u32[]{:S(2)}) collective-permute-start(bf16[1,2,128]{2,1,0:T(2,128)(2,1)S(1)} %get-tuple-element.20), channel_id=1, source_target_pairs={{0,4},{4,8},{8,12},{12,16},{16,20},{20,24},{24,28},{28,32},{32,36}... | collective-permute-start | bytes 1544 | tf_op jit(solution)/shard_map/ppermute | solution.py:285
  24.2 0.9 copy-start.1
  25.1 0.8 copy-start.3
  25.9 0.7 copy-start.7
  26.5 0.7 copy-start.8
  28.4 0.9 copy-start.2
  29.3 0.7 copy-start.6
  30.0 0.7 copy-start.10
  30.6 45.4 %copy-start.4 = (s32[64,128]{1,0:T(8,128)S(1)}, s32[64,128]{1,0:T(8,128)}, u32[]{:S(2)}) copy-start(s32[64,128]{1,0:T(8,128)} %skel_ref.4) | copy-start | bytes 98308
  33.3 33.0 %all-to-all-start = ((bf16[640,2,128]{2,1,0:T(2,128)(2,1)}), bf16[640,2,128]{2,1,0:T(2,128)(2,1)S(1)}, u32[]{:S(2)}, u32[]{:S(2)}) async-start(bf16[640,2,128]{2,1,0:T(2,128)(2,1)} %bitcast.2), calls=%async_computation | async-start | bytes 655360 | tf_op jit(solution)/shard_map/all_to_all | solution.py:311
  66.2 1.3 %copy-start = (f32[2560,128]{1,0:T(8,128)S(1)}, f32[2560,128]{1,0:T(8,128)}, u32[]{:S(2)}) copy-start(f32[2560,128]{1,0:T(8,128)} %all-gather.3.cloned.1.call-done) | copy-start | bytes 3932164
  71.2 4.9 %collective-permute-start.4 = (f32[128,512]{1,0:T(8,128)S(1)}, f32[128,512]{1,0:T(8,128)S(1)}, u32[]{:S(2)}, u32[]{:S(2)}) collective-permute-start(f32[128,512]{1,0:T(8,128)S(1)} %get-tuple-element.14.own_ref.chosen_ref), channel_id=1, source_target_pairs={{0,4},{4,0},{8,12},{12,8},{16,20},{20,16},{24,28},{28,24},{32,36},... | collective-permute-start | bytes 786440 | tf_op jit(solution)/shard_map/ppermute | solution.py:290
  77.1 19.0 %collective-permute-start.5 = (f32[128,512]{1,0:T(8,128)S(1)}, f32[128,512]{1,0:T(8,128)S(1)}, u32[]{:S(2)}, u32[]{:S(2)}) collective-permute-start(f32[128,512]{1,0:T(8,128)S(1)} %pair.1.pair_ref.own_ref), channel_id=1, source_target_pairs={{0,8},{4,12},{8,0},{12,4},{16,24},{20,28},{24,16},{28,20},{32,40},... | collective-permute-start | bytes 786440 | tf_op jit(solution)/shard_map/ppermute | solution.py:290
  79.3 16.8 %copy-start.5 = (s32[32,128]{1,0:T(8,128)S(1)}, s32[32,128]{1,0:T(8,128)}, u32[]{:S(2)}) copy-start(s32[32,128]{1,0:T(8,128)} %skel_ref.5) | copy-start | bytes 49156
Sparse Core Ops, SparseCore 0:
  28.5 33.5 all-gather.2

commit v2 on v1

v2 whole, which is shorter than its diff:
```python
import functools

import jax
import jax.numpy as jnp
from jax import lax
from jax.experimental import pallas as pl
from jax.experimental.pallas import tpu as pltpu
from jax.sharding import PartitionSpec as P

LINE = 512
CAP = 8
SLOT = CAP + 2
RANK = 128
ROWS = 256
HIGHEST = lax.Precision.HIGHEST
F32 = jnp.float32
BF16 = jnp.bfloat16
VMEM_LIMIT = 24 * 1024 * 1024
VMEM_ALL = 60 * 1024 * 1024


def whole(value):
    return pl.BlockSpec(value.shape, lambda: (0,) * value.ndim)


def iota(shape, dim):
    return lax.broadcasted_iota(jnp.int32, shape, dim)


def column_of(row):
    square = jnp.broadcast_to(row, (128, 128))
    return jnp.sum(jnp.where(iota((128, 128), 0) == iota((128, 128), 1), square, jnp.zeros_like(square)), 1, keepdims=True)


def side_by_side(ref):
    return jnp.concatenate([ref[s] for s in range(ref.shape[0])], 1)


def dot(a, b, dims=(((1,), (0,)), ((), ())), precision=None):
    return lax.dot_general(a, b, dims, precision=precision, preferred_element_type=F32)


ROW_ROW = (((1,), (1,)), ((), ()))
COL_COL = (((0,), (0,)), ((), ()))


def route_kernel(of_ref, map_ref, gen_ref, out_ref):
    blocks = map_ref.shape[0]
    count = blocks * 128
    targets = map_ref[...]
    owner = lax.shift_right_arithmetic(targets, 8)
    place = (targets & (ROWS - 1)) + 1
    owner_row = jnp.concatenate([owner[b : b + 1] for b in range(blocks)], 1).astype(F32)
    owner_col = jnp.concatenate([column_of(owner[b : b + 1].astype(F32)) for b in range(blocks)], 0)
    place_col = jnp.concatenate([column_of(place[b : b + 1].astype(F32)) for b in range(blocks)], 0)
    label_col = jnp.concatenate([jnp.full((128, 1), of_ref[b], jnp.int32) for b in range(blocks)], 0).astype(F32)
    same = jnp.where(owner_col == owner_row, 1.0, 0.0)
    sub, lane = iota((count, count), 0), iota((count, count), 1)
    within_row = jnp.sum(jnp.where(sub < lane, same, 0.0), 0, keepdims=True)
    within_col = jnp.sum(jnp.where(lane < sub, same, 0.0), 1, keepdims=True)
    slot_row = jnp.where(owner_row >= 0, owner_row * SLOT + within_row, -1.0).astype(jnp.int32)
    info_row = jnp.where(owner_row >= 0, owner_row * SLOT + CAP, -1.0).astype(jnp.int32)
    lanes = iota((count, 128), 1)
    within_at = within_col.astype(jnp.int32)
    info = jnp.where(lanes == within_at, place_col, 0.0) + jnp.where(lanes == within_at + CAP, label_col, 0.0)
    table = jnp.concatenate([gen_ref[...], info.astype(BF16)], 0)
    rows = out_ref.shape[0]
    step = min(256, rows)
    for first in range(0, rows, step):
        at = iota((step, count), 0) + first
        pick = jnp.concatenate([jnp.where(at == slot_row, 1.0, 0.0), jnp.where(at == info_row, 1.0, 0.0)], 1)
        out_ref[first : first + step] = dot(pick.astype(BF16), table).astype(BF16)


def route(child_map, child_of, child_gen, devices):
    return pl.pallas_call(
        route_kernel,
        out_shape=jax.ShapeDtypeStruct((devices * SLOT, child_gen.shape[1]), BF16),
        in_specs=[pl.BlockSpec(memory_space=pltpu.SMEM), whole(child_map), whole(child_gen)],
        out_specs=pl.BlockSpec(memory_space=pltpu.VMEM),
        compiler_params=pltpu.CompilerParams(vmem_limit_bytes=VMEM_ALL),
        name="route",
    )(child_of, child_map, child_gen)


def one_hot(skel_ref, group, width, shift=0):
    picks = column_of(skel_ref[pl.ds(group, 1), :].astype(F32)).astype(jnp.int32)
    return jnp.where(iota((RANK, width), 1) == ((picks + shift) & (width - 1)), 1.0, 0.0)


def child_kernel(
    where_ref, got_ref, coef_ref, x_ref, real_ref, imag_ref, leaf_skel_ref, pair_skel_ref, quad_skel_ref,
    out_ref, leaf_pick_ref, pair_pick_ref, quad_pick_ref,
):
    position = where_ref[0]
    low, high = position & 1, lax.shift_right_arithmetic(position, 1) & 1
    leaf_pick_ref[...] = one_hot(leaf_skel_ref, 0, 2 * ROWS)
    pair_pick_ref[...] = one_hot(pair_skel_ref, lax.shift_right_arithmetic(position, 1), 2 * RANK, RANK * low)
    quad_pick_ref[...] = one_hot(quad_skel_ref, lax.shift_right_arithmetic(position, 2), 2 * RANK, RANK * high)
    rows = 2 * ROWS
    sub_x = iota((rows, 128), 0)
    half = lax.shift_right_arithmetic(iota((256, 128), 0), 1) == iota((256, 128), 1)

    def spread_rows(ref):
        blocks = [jnp.sum(jnp.where(half, ref[b : b + 1, :], 0.0), 1, keepdims=True) for b in range(ref.shape[0])]
        return jnp.concatenate(blocks, 0)

    real, imag = spread_rows(real_ref) + 4.0, spread_rows(imag_ref)
    got = got_ref[...]
    count = got.shape[0]
    sources = count // SLOT
    info_at = iota((sources, count), 0) * SLOT + CAP == iota((sources, count), 1)
    info = dot(jnp.where(info_at, 1.0, 0.0).astype(BF16), got).astype(BF16)
    along = iota((count, sources), 0)
    source = lax.shift_right_arithmetic(along * 6554, 16)
    spread = dot(jnp.where(source == iota((count, sources), 1), 1.0, 0.0).astype(BF16), info)
    sub = iota((count, 128), 0)
    slot = sub - SLOT * lax.shift_right_arithmetic(sub * 6554, 16)
    label = jnp.sum(jnp.where(iota((count, 128), 1) == slot + CAP, spread, 0.0), 1, keepdims=True)
    along_t = iota((sources, count), 1)
    source_t = lax.shift_right_arithmetic(along_t * 6554, 16)
    spread_t = dot(info, jnp.where(source_t == iota((sources, count), 0), 1.0, 0.0).astype(BF16), COL_COL)
    lane = iota((128, count), 1)
    slot_t = lane - SLOT * lax.shift_right_arithmetic(lane * 6554, 16)
    sub_t = iota((128, count), 0)
    code = jnp.sum(jnp.where((sub_t == slot_t) & (sub_t < CAP), spread_t, 0.0), 0, keepdims=True)
    onto = jnp.where(iota((ROWS, count), 0) + 1 == code.astype(jnp.int32), 1.0, 0.0).astype(BF16)
    wide = got.astype(F32)
    zero = jnp.zeros_like(wide)
    parts = jnp.concatenate([jnp.where(label == 0.0, wide, zero), jnp.where(label == 0.0, zero, wide)], 1).astype(BF16)
    rank = coef_ref.shape[1] // 2
    for s in range(coef_ref.shape[0]):
        coef = coef_ref[s]
        first, second, none = coef[:rank], coef[rank:], jnp.zeros((rank, 128), BF16)
        table = jnp.concatenate(
            [jnp.concatenate([first, none, second, none], 0), jnp.concatenate([none, first, none, second], 0)], 1
        )
        values = dot(parts, table).astype(BF16)
        sums = dot(onto, values)
        for c in range(2):
            out_ref[s, pl.ds(c, ROWS, stride=2), :] = sums[:, c * 128 : (c + 1) * 128]
        x = x_ref[s].astype(F32)
        before = jnp.where(sub_x < 2, 0.0, pltpu.roll(x, 2, 0))
        after = jnp.where(sub_x >= rows - 2, 0.0, pltpu.roll(x, rows - 2, 0))
        turned = jnp.where((sub_x & 1) == 0, -pltpu.roll(x, rows - 1, 0), pltpu.roll(x, 1, 0))
        out_ref[s] = out_ref[s] + (real * x + imag * turned - (before + after))


def child(where, got, coef, x, *others):
    return pl.pallas_call(
        child_kernel,
        out_shape=[
            jax.ShapeDtypeStruct((coef.shape[0], 2 * ROWS, coef.shape[2]), F32),
            jax.ShapeDtypeStruct((RANK, 2 * ROWS), F32),
            jax.ShapeDtypeStruct((RANK, 2 * RANK), F32),
            jax.ShapeDtypeStruct((RANK, 2 * RANK), F32),
        ],
        in_specs=[pl.BlockSpec(memory_space=pltpu.SMEM)]
        + [pl.BlockSpec(memory_space=pltpu.VMEM)] * 3
        + [whole(value) for value in others],
        out_specs=[pl.BlockSpec(memory_space=pltpu.VMEM)] * 4,
        cost_estimate=pl.CostEstimate(flops=2_000_000_000, bytes_accessed=2_000_000, transcendentals=0),
        compiler_params=pltpu.CompilerParams(vmem_limit_bytes=VMEM_LIMIT),
        name="child",
    )(where, got, coef, x, *others)


def leaf_kernel(where_ref, part_ref, low_ref, high_ref, left_ref, right_ref, pick_ref, own_ref, leaf_ref, chosen_ref):
    parts, rows, width = part_ref.shape
    sub = iota((8, width), 0)
    for s in range(parts):
        left, right = left_ref[s].astype(F32), right_ref[s].astype(F32)
        leaf_ref[s] = part_ref[s] - (low_ref[s].astype(F32) + high_ref[s].astype(F32))
        first = jnp.where(sub == 0, left[0:1], jnp.where(sub == 1, left[1:2], 0.0))
        last = jnp.where(sub == 6, right[0:1], jnp.where(sub == 7, right[1:2], 0.0))
        leaf_ref[s, 0:8, :] = leaf_ref[s, 0:8, :] - first
        leaf_ref[s, rows - 8 : rows, :] = leaf_ref[s, rows - 8 : rows, :] - last
    own_ref[...] = leaf_ref[where_ref[1]]
    chosen_ref[...] = dot(pick_ref[...], side_by_side(leaf_ref), precision=HIGHEST)


def leaf(where, part, *others):
    parts, rows, width = part.shape
    return pl.pallas_call(
        leaf_kernel,
        out_shape=[
            jax.ShapeDtypeStruct((rows, width), F32),
            jax.ShapeDtypeStruct(part.shape, F32),
            jax.ShapeDtypeStruct((RANK, parts * width), F32),
        ],
        in_specs=[pl.BlockSpec(memory_space=pltpu.SMEM)] + [pl.BlockSpec(memory_space=pltpu.VMEM)] * 6,
        out_specs=[pl.BlockSpec(memory_space=pltpu.VMEM)] * 3,
        compiler_params=pltpu.CompilerParams(vmem_limit_bytes=VMEM_LIMIT),
        name="leaf",
    )(where, part, *others)


def products_kernel(leaf_ref, chosen_ref, gram_ref, cross_ref):
    chosen = chosen_ref[...]
    gram_ref[...] = dot(chosen, chosen, ROW_ROW, HIGHEST)
    cross_ref[...] = dot(side_by_side(leaf_ref), chosen, ROW_ROW, HIGHEST)


def products(leaf_rows, chosen):
    return pl.pallas_call(
        products_kernel,
        out_shape=[
            jax.ShapeDtypeStruct((RANK, RANK), F32),
            jax.ShapeDtypeStruct((leaf_rows.shape[1], RANK), F32),
        ],
        in_specs=[pl.BlockSpec(memory_space=pltpu.VMEM)] * 2,
        out_specs=[pl.BlockSpec(memory_space=pltpu.VMEM)] * 2,
        cost_estimate=pl.CostEstimate(flops=1_000_000_000, bytes_accessed=2_000_000, transcendentals=0),
        compiler_params=pltpu.CompilerParams(vmem_limit_bytes=VMEM_LIMIT),
        name="products",
    )(leaf_rows, chosen)


def pair_kernel(pick_ref, own_ref, other_ref, out_ref):
    out_ref[...] = dot(pick_ref[...], jnp.concatenate([own_ref[...], other_ref[...]], 0), precision=HIGHEST)


def pair(pick, own, other):
    return pl.pallas_call(
        pair_kernel,
        out_shape=jax.ShapeDtypeStruct(own.shape, F32),
        in_specs=[pl.BlockSpec(memory_space=pltpu.VMEM)] * 3,
        out_specs=pl.BlockSpec(memory_space=pltpu.VMEM),
        compiler_params=pltpu.CompilerParams(vmem_limit_bytes=VMEM_LIMIT),
        name="pair",
    )(pick, own, other)


def invert_in_place(refs, width=32):
    sub = iota((8, RANK), 0)
    lane = iota((8, RANK), 1)
    wide_lane = iota((width, RANK), 1)
    count, panels = width // 8, RANK // width
    matrices = [[ref[8 * m : 8 * m + 8, :] for m in range(RANK // 8)] for ref in refs]

    def eliminated(panel, at, j):
        inside = (lane >= at) & (lane < at + 8)

        def along(block, k):
            return jnp.take_along_axis(block, jnp.full((8, RANK), at + k, jnp.int32), axis=1)

        columns = [along(panel[j], k) for k in range(8)]
        block = jnp.where(inside, jnp.where(lane - at == sub, 1.0, 0.0), panel[j])
        for i in range(8):
            minus = jnp.where(sub == i, columns[i] - 1.0, columns[i]) * (1.0 / columns[i][i : i + 1, :])
            block = block - minus * block[i : i + 1, :]
            for k in range(i + 1, 8):
                columns[k] = columns[k] - minus * columns[k][i : i + 1, :]
        result = []
        for m in range(count):
            total = block
            if m != j:
                total = jnp.where(inside, 0.0, panel[m])
                for k in range(8):
                    total = total - along(panel[m], k) * block[k : k + 1, :]
            result.append(total)
        return result

    for p in range(panels):
        base = p * width
        inside = (wide_lane >= base) & (wide_lane < base + width)
        for matrix in matrices:
            panel = matrix[p * count : (p + 1) * count]
            for j in range(count):
                panel = eliminated(panel, base + 8 * j, j)
            rows = jnp.concatenate(panel, 0)
            for q in [(p + 1 + t) % panels for t in range(panels - 1)]:
                old = jnp.concatenate(matrix[q * count : (q + 1) * count], 0)
                new = jnp.where(inside, 0.0, old) - dot(old[:, base : base + width], rows, precision=HIGHEST)
                for j in range(count):
                    matrix[q * count + j] = new[8 * j : 8 * j + 8, :]
            matrix[p * count : (p + 1) * count] = panel
    for ref, matrix in zip(refs, matrices):
        for m in range(RANK // 8):
            ref[8 * m : 8 * m + 8, :] = matrix[m]


def applied(cross, gram, inverse):
    unit = jnp.where(iota((RANK, RANK), 0) == iota((RANK, RANK), 1), 1.0, 0.0)
    rough = dot(cross, inverse, precision=HIGHEST)
    return rough + dot(rough, unit - dot(gram, inverse, precision=HIGHEST), precision=HIGHEST)


def interp_kernel(leaf_gram_ref, leaf_cross_ref, chosen_ref, upper_ref, leaf_out, merge_out, first, second):
    upper = upper_ref[...]
    merge_gram = dot(upper, upper, ROW_ROW, HIGHEST)
    first[...] = leaf_gram_ref[...]
    second[...] = merge_gram
    invert_in_place([first, second])
    merge_cross = dot(chosen_ref[...], upper, ROW_ROW, HIGHEST)
    leaf_out[...] = applied(leaf_cross_ref[...], leaf_gram_ref[...], first[...])
    merge_out[...] = applied(merge_cross, merge_gram, second[...])


def interp(leaf_gram, leaf_cross, chosen, upper):
    return pl.pallas_call(
        interp_kernel,
        out_shape=[
            jax.ShapeDtypeStruct(leaf_cross.shape, F32),
            jax.ShapeDtypeStruct((RANK, RANK), F32),
        ],
        in_specs=[pl.BlockSpec(memory_space=pltpu.VMEM)] * 4,
        out_specs=[pl.BlockSpec(memory_space=pltpu.VMEM)] * 2,
        scratch_shapes=[pltpu.VMEM((RANK, RANK), F32)] * 2,
        cost_estimate=pl.CostEstimate(flops=8_000_000_000, bytes_accessed=2_000_000, transcendentals=0),
        compiler_params=pltpu.CompilerParams(vmem_limit_bytes=VMEM_LIMIT),
        name="interp",
    )(leaf_gram, leaf_cross, chosen, upper)


def top_kernel(where_ref, pick_ref, own_ref, other_ref, top_out, rows_out, gram, quad):
    position = where_ref[0]
    chosen = dot(pick_ref[...], jnp.concatenate([own_ref[...], other_ref[...]], 0), precision=HIGHEST)
    quad[...] = chosen
    top_gram = dot(chosen, chosen, ROW_ROW, HIGHEST)
    gram[...] = top_gram
    columns = pl.ds(pl.multiple_of(where_ref[1] * 128, 128), 128)
    rows_out[...] = quad[pl.ds(pl.multiple_of((position & 3) * (RANK // 4), RANK // 4), RANK // 4), columns]
    invert_in_place([gram], 64)
    own = own_ref[pl.ds(pl.multiple_of((position & 1) * (RANK // 2), RANK // 2), RANK // 2), :]
    top_out[...] = applied(dot(own, chosen, ROW_ROW, HIGHEST), top_gram, gram[...])


def top(where, pick, own, other):
    return pl.pallas_call(
        top_kernel,
        out_shape=[jax.ShapeDtypeStruct((RANK // 2, RANK), F32), jax.ShapeDtypeStruct((RANK // 4, 128), F32)],
        in_specs=[pl.BlockSpec(memory_space=pltpu.SMEM)] + [pl.BlockSpec(memory_space=pltpu.VMEM)] * 3,
        out_specs=[pl.BlockSpec(memory_space=pltpu.VMEM)] * 2,
        scratch_shapes=[pltpu.VMEM((RANK, RANK), F32), pltpu.VMEM(own.shape, F32)],
        compiler_params=pltpu.CompilerParams(vmem_limit_bytes=VMEM_LIMIT),
        name="top",
    )(where, pick, own, other)


def shifted(value, axis, steps):
    count = lax.axis_size(axis)
    first, last = (max(0, -steps), min(count, count - steps))
    return lax.ppermute(value, axis, [(source, source + steps) for source in range(first, last)])


def swapped(block, axis, apart):
    count = lax.axis_size(axis)
    return lax.ppermute(block, axis, [(i, i ^ (1 << apart)) for i in range(count)])


def body(
    probe, shift_real, shift_imag, child_gen, child_coef, child_map, child_of, leaf_skel, pair_skel, quad_skel
):
    row_count, _, col_count = probe.shape
    devices = lax.axis_size("row")
    where = jnp.stack([lax.axis_index("row"), lax.axis_index("samp")]).astype(jnp.int32)
    offset = LINE // row_count
    everyone = lax.all_gather(
        jnp.concatenate([probe.reshape(-1, col_count), child_coef.reshape(-1, col_count)], 0), "samp"
    )
    wide, coef = everyone[:, : 2 * row_count], everyone[:, 2 * row_count :]
    outgoing = route(child_map, child_of, child_gen, devices)
    got = lax.all_to_all(
        outgoing.reshape(devices * SLOT // 2, 2, -1), "row", split_axis=0, concat_axis=0, tiled=True
    ).reshape(devices * SLOT, -1)
    low = shifted(wide, "row", offset)
    high = shifted(wide, "row", -offset)
    left = shifted(wide[:, -2:], "row", 1)
    right = shifted(wide[:, :2], "row", -1)
    part, leaf_pick, pair_pick, quad_pick = child(
        where, got, coef, wide, shift_real.reshape(-1, 128), shift_imag.reshape(-1, 128),
        leaf_skel, pair_skel, quad_skel,
    )
    own, leaf_rows, chosen = leaf(where, part, low, high, left, right, leaf_pick)
    leaf_gram, leaf_cross = products(leaf_rows, chosen)
    upper = pair(pair_pick, chosen, swapped(chosen, "row", 0))
    leaf_interp, merge_interp = interp(leaf_gram, leaf_cross, chosen, upper)
    top_interp, top_rows = top(where, quad_pick, upper, swapped(upper, "row", 1))
    return own.reshape(row_count, 2, col_count), leaf_interp, merge_interp, top_interp, top_rows


def solution(mesh):
    return jax.shard_map(
        body,
        mesh=mesh,
        in_specs=(
            P("row", None, "samp"),
            P("row"),
            P("row"),
            P("row", None),
            P(None, None, "samp"),
            P("row", None),
            P("row"),
            P("row", None),
            P(),
            P(),
        ),
        out_specs=(
            P("row", None, "samp"),
            P("row", None),
            P("row", None),
            P("row", None),
            P("row", "samp"),
        ),
        check_vma=False,
    )
```

time: 113 us -> 80 us (0.71)
  the two profiles are of different devices: /device:TPU:1 before, /device:TPU:32 now
where the time goes in v2:
time: 80 us; the launch traced here: 79.6 us
  starting transfers between devices  34.6 us (43%)
  Pallas kernels  24 us (30%)
  blocking collectives  13.5 us (17%)
  waiting for transfers between devices  5.94 us (7%)
  between operations  0.8 us (1%)
    all_to_all x1, starting transfers between devices, body(): lax.all_to_all(outgoing.reshape(devices * SLOT // 2, 2, -1), 'row', split...  17.5 us
    all_gather x1, blocking collectives, body(): lax.all_gather(jnp.concatenate([probe.reshape(-1, col_count), child_coef....  13.5 us
    ppermute x4, starting transfers between devices, shifted(): lax.ppermute(value, axis, [(source, source + steps) for source in range(f...  13.1 us
    pallas_call x1, Pallas kernels, top(): pl.pallas_call(top_kernel, out_shape=[jax.ShapeDtypeStruct((RANK // 2, RA...  7.15 us
    pallas_call x1, Pallas kernels, interp(): pl.pallas_call(interp_kernel, out_shape=[jax.ShapeDtypeStruct(leaf_cross....  6.99 us
    ppermute x4, waiting for transfers between devices, shifted(): lax.ppermute(value, axis, [(source, source + steps) for source in range(f...  4.43 us
    ppermute x2, starting transfers between devices, swapped(): lax.ppermute(block, axis, [(i, i ^ 1 << apart) for i in range(count)])  4.01 us
    pallas_call x1, Pallas kernels, child(): pl.pallas_call(child_kernel, out_shape=[jax.ShapeDtypeStruct((coef.shape[...  3.34 us
  transfers between devices with their start and end apart: 7, of which 4 were waited for; matrix products, arithmetic and copies ran while one was open for 0% of the time, Pallas kernels for 14%

profile of v2, /device:TPU:32, one launch (start us, length us, event | category | flops | bytes accessed | tf_op | source)
XLA Modules:
  0.0 79.6 jit_solution(16719742654379848803)
XLA Ops:
  0.6 3.0 %route.1 = bf16[1280,128]{1,0:T(8,128)(2,1)} custom-call(s32[4]{0:T(128)} %of_ref.1, s32[4,128]{1,0:T(4,128)} %map_ref.1, bf16[512,128]{1,0:T(8,128)(2,1)} %gen_ref.1), custom_call_target="tpu_custom_call" | custom-call | tf_op jit(solution)/shard_map/route/pallas_call | solution.py:76
  3.6 17.5 %all-to-all-start = ((bf16[640,2,128]{2,1,0:T(2,128)(2,1)}), bf16[640,2,128]{2,1,0:T(2,128)(2,1)S(1)}, u32[]{:S(2)}, u32[]{:S(2)}) async-start(bf16[640,2,128]{2,1,0:T(2,128)(2,1)} %bitcast.16), calls=%async_computation | async-start | bytes 655360 | tf_op jit(solution)/shard_map/all_to_all | solution.py:364
  21.1 0.0 copy-done.5
  21.1 0.0 copy-done.6
  21.1 13.5 %all-gather = bf16[2560,128]{1,0:T(8,128)(2,1)S(1)} all-gather(bf16[640,128]{1,0:T(8,128)(2,1)S(1)} %pad_maximum_fusion), channel_id=2, replica_groups=mesh['row'=128,'samp'=4] {'samp'}, dimensions={0}, use_global_device_ids=true | all-gather | bytes 819200 | tf_op jit(solution)/shard_map/all_gather | solution.py:359
  34.6 4.6 %collective-permute-start.1 = (bf16[4,512,128]{2,1,0:T(8,128)(2,1)S(1)}, bf16[4,512,128]{2,1,0:T(8,128)(2,1)S(1)}, u32[]{:S(2)}, u32[]{:S(2)}) collective-permute-start(bf16[4,512,128]{2,1,0:T(8,128)(2,1)S(1)} %slice.19.x_ref), channel_id=1, source_target_pairs={{8,0},{12,4},{16,8},{20,12},{24,16},{28,20},{32,24},{36,28},{40,32... | collective-permute-start | bytes 1572872 | tf_op jit(solution)/shard_map/ppermute | solution.py:344
  39.2 1.9 %collective-permute-start = (bf16[4,512,128]{2,1,0:T(8,128)(2,1)S(1)}, bf16[4,512,128]{2,1,0:T(8,128)(2,1)S(1)}, u32[]{:S(2)}, u32[]{:S(2)}) collective-permute-start(bf16[4,512,128]{2,1,0:T(8,128)(2,1)S(1)} %slice.19.x_ref), channel_id=1, source_target_pairs={{0,8},{4,12},{8,16},{12,20},{16,24},{20,28},{24,32},{28,36},{32,40... | collective-permute-start | bytes 1572872 | tf_op jit(solution)/shard_map/ppermute | solution.py:344
  41.1 4.7 %collective-permute-start.3 = (bf16[4,2,128]{2,1,0:T(2,128)(2,1)S(1)}, bf16[4,2,128]{2,1,0:T(2,128)(2,1)S(1)}, u32[]{:S(2)}, u32[]{:S(2)}) collective-permute-start(bf16[4,2,128]{2,1,0:T(2,128)(2,1)S(1)} %get-tuple-element.31), channel_id=1, source_target_pairs={{4,0},{8,4},{12,8},{16,12},{20,16},{24,20},{28,24},{32,28},{36,32}... | collective-permute-start | bytes 6152 | tf_op jit(solution)/shard_map/ppermute | solution.py:344
  45.8 1.9 %collective-permute-start.2 = (bf16[4,2,128]{2,1,0:T(2,128)(2,1)S(1)}, bf16[4,2,128]{2,1,0:T(2,128)(2,1)S(1)}, u32[]{:S(2)}, u32[]{:S(2)}) collective-permute-start(bf16[4,2,128]{2,1,0:T(2,128)(2,1)S(1)} %get-tuple-element.32), channel_id=1, source_target_pairs={{0,4},{4,8},{8,12},{12,16},{16,20},{20,24},{24,28},{28,32},{32,36}... | collective-permute-start | bytes 6152 | tf_op jit(solution)/shard_map/ppermute | solution.py:344
  47.8 0.0 copy-start
  47.8 0.0 copy-start.3
  47.8 0.0 copy-start.1
  47.8 0.1 pad_add_fusion.where_ref
  47.9 0.0 all-to-all-done
  47.9 0.6 copy-done
  48.5 0.0 copy-done.1
  48.5 0.1 copy-done.2
  48.6 0.0 copy-done.4
  48.6 3.3 %child.1 = (f32[4,512,128]{2,1,0:T(8,128)S(1)}, f32[128,512]{1,0:T(8,128)S(1)}, f32[128,256]{1,0:T(8,128)S(1)}, f32[128,256]{1,0:T(8,128)S(1)}) custom-call(s32[2]{0:T(128)S(1)} %pad_add_fusion.where_ref, bf16[1280,128]{1,0:T(8,128)(2,1)S(1)} %bitcast.10, bf16[4,128,128]{2,1,0:T(8,128)(2,1)S(1)} %slice.18.coef_ref, bf16[4,512,128]{2,1,0:T(8,128)(2,1)S(1)} %slice.19.x_ref, ...), custom_call_target="tpu_custom_call" | custom-call | flops 2000000000 | bytes 2000000 | tf_op jit(solution)/shard_map/child/pallas_call | solution.py:150
  52.0 0.0 collective-permute-done.3.right_ref
  52.0 2.2 %collective-permute-done.2.left_ref = bf16[4,2,128]{2,1,0:T(2,128)(2,1)S(1)} collective-permute-done((bf16[4,2,128]{2,1,0:T(2,128)(2,1)S(1)}, bf16[4,2,128]{2,1,0:T(2,128)(2,1)S(1)}, u32[]{:S(2)}, u32[]{:S(2)}) %collective-permute-start.2) | collective-permute-done | bytes 2080 | tf_op jit(solution)/shard_map/ppermute | solution.py:344
  54.2 0.0 collective-permute-done.1.high_ref
  54.2 2.2 %collective-permute-done.low_ref = bf16[4,512,128]{2,1,0:T(8,128)(2,1)S(1)} collective-permute-done((bf16[4,512,128]{2,1,0:T(8,128)(2,1)S(1)}, bf16[4,512,128]{2,1,0:T(8,128)(2,1)S(1)}, u32[]{:S(2)}, u32[]{:S(2)}) %collective-permute-start) | collective-permute-done | bytes 524320 | tf_op jit(solution)/shard_map/ppermute | solution.py:344
  56.4 1.9 %leaf.1 = (f32[512,128]{1,0:T(8,128)}, f32[4,512,128]{2,1,0:T(8,128)S(1)}, f32[128,512]{1,0:T(8,128)S(1)}) custom-call(s32[2]{0:T(128)S(1)} %pad_add_fusion.where_ref, f32[4,512,128]{2,1,0:T(8,128)S(1)} %get-tuple-element.18.part_ref, bf16[4,512,128]{2,1,0:T(8,128)(2,1)S(1)} %collective-permute-done.low_ref, ...), custom_call_target="tpu_custom_call" | custom-call | tf_op jit(solution)/shard_map/leaf/pallas_call | solution.py:184
  58.3 1.9 %collective-permute-start.4 = (f32[128,512]{1,0:T(8,128)S(1)}, f32[128,512]{1,0:T(8,128)S(1)}, u32[]{:S(2)}, u32[]{:S(2)}) collective-permute-start(f32[128,512]{1,0:T(8,128)S(1)} %get-tuple-element.22.chosen_ref.own_ref), channel_id=1, source_target_pairs={{0,4},{4,0},{8,12},{12,8},{16,20},{20,16},{24,28},{28,24},{32,36},... | collective-permute-start | bytes 786440 | tf_op jit(solution)/shard_map/ppermute | solution.py:349
  60.2 1.2 %products.1 = (f32[128,128]{1,0:T(8,128)S(1)}, f32[512,128]{1,0:T(8,128)S(1)}) custom-call(f32[4,512,128]{2,1,0:T(8,128)S(1)} %get-tuple-element.21.leaf_ref, f32[128,512]{1,0:T(8,128)S(1)} %get-tuple-element.22.chosen_ref.own_ref), custom_call_target="tpu_custom_call" | custom-call | flops 1000000000 | bytes 2000000 | tf_op jit(solution)/shard_map/products/pallas_call | solution.py:205
  61.4 0.3 collective-permute-done.4.other_ref
  61.7 0.4 pair.1.upper_ref.own_ref
  62.1 2.1 %collective-permute-start.5 = (f32[128,512]{1,0:T(8,128)S(1)}, f32[128,512]{1,0:T(8,128)S(1)}, u32[]{:S(2)}, u32[]{:S(2)}) collective-permute-start(f32[128,512]{1,0:T(8,128)S(1)} %pair.1.upper_ref.own_ref), channel_id=1, source_target_pairs={{0,8},{4,12},{8,0},{12,4},{16,24},{20,28},{24,16},{28,20},{32,40},... | collective-permute-start | bytes 786440 | tf_op jit(solution)/shard_map/ppermute | solution.py:349
  64.3 7.0 %interp.1 = (f32[512,128]{1,0:T(8,128)}, f32[128,128]{1,0:T(8,128)}) custom-call(f32[128,128]{1,0:T(8,128)S(1)} %get-tuple-element.23.leaf_gram_ref, f32[512,128]{1,0:T(8,128)S(1)} %get-tuple-element.24.leaf_cross_ref, f32[128,512]{1,0:T(8,128)S(1)} %get-tuple-element.22.chosen_ref.own_ref, f32[128,512]{1,0:T(8,128)S(1)} %pair.1.upper_ref.own_ref), custom_call_target="tpu_custom_call" | custom-call | flops 8000000000 | bytes 2000000 | tf_op jit(solution)/shard_map/interp/pallas_call | solution.py:301
  71.2 1.2 %collective-permute-done.5.other_ref = f32[128,512]{1,0:T(8,128)S(1)} collective-permute-done((f32[128,512]{1,0:T(8,128)S(1)}, f32[128,512]{1,0:T(8,128)S(1)}, u32[]{:S(2)}, u32[]{:S(2)}) %collective-permute-start.5) | collective-permute-done | bytes 262176 | tf_op jit(solution)/shard_map/ppermute | solution.py:349
  72.5 7.2 %top.1 = (f32[64,128]{1,0:T(8,128)}, f32[32,128]{1,0:T(8,128)}) custom-call(s32[2]{0:T(128)S(1)} %pad_add_fusion.where_ref, f32[128,256]{1,0:T(8,128)S(1)} %get-tuple-element.28.pick_ref, f32[128,512]{1,0:T(8,128)S(1)} %pair.1.upper_ref.own_ref, f32[128,512]{1,0:T(8,128)S(1)} %collective-permute-done.5.other_ref), custom_call_target="tpu_custom_call" | custom-call | tf_op jit(solution)/shard_map/top/pallas_call | solution.py:330
  (9 shorter events, 0.1 us)
Async XLA Ops:
  3.6 17.5 %copy-start.5 = (bf16[256,2,128]{2,1,0:T(2,128)(2,1)S(1)}, bf16[256,2,128]{2,1,0:T(2,128)(2,1)}, u32[]{:S(2)}) copy-start(bf16[256,2,128]{2,1,0:T(2,128)(2,1)} %param.10) | copy-start | bytes 393220
  3.6 17.5 %copy-start.6 = (bf16[2,64,128]{2,1,0:T(8,128)(2,1)S(1)}, bf16[2,64,128]{2,1,0:T(8,128)(2,1)}, u32[]{:S(2)}) copy-start(bf16[2,64,128]{2,1,0:T(8,128)(2,1)} %param.14) | copy-start | bytes 98308
  3.6 44.3 %all-to-all-start = ((bf16[640,2,128]{2,1,0:T(2,128)(2,1)}), bf16[640,2,128]{2,1,0:T(2,128)(2,1)S(1)}, u32[]{:S(2)}, u32[]{:S(2)}) async-start(bf16[640,2,128]{2,1,0:T(2,128)(2,1)} %bitcast.16), calls=%async_computation | async-start | bytes 655360 | tf_op jit(solution)/shard_map/all_to_all | solution.py:364
  34.6 19.5 %collective-permute-start.1 = (bf16[4,512,128]{2,1,0:T(8,128)(2,1)S(1)}, bf16[4,512,128]{2,1,0:T(8,128)(2,1)S(1)}, u32[]{:S(2)}, u32[]{:S(2)}) collective-permute-start(bf16[4,512,128]{2,1,0:T(8,128)(2,1)S(1)} %slice.19.x_ref), channel_id=1, source_target_pairs={{8,0},{12,4},{16,8},{20,12},{24,16},{28,20},{32,24},{36,28},{40,32... | collective-permute-start | bytes 1572872 | tf_op jit(solution)/shard_map/ppermute | solution.py:344
  39.2 17.2 %collective-permute-start = (bf16[4,512,128]{2,1,0:T(8,128)(2,1)S(1)}, bf16[4,512,128]{2,1,0:T(8,128)(2,1)S(1)}, u32[]{:S(2)}, u32[]{:S(2)}) collective-permute-start(bf16[4,512,128]{2,1,0:T(8,128)(2,1)S(1)} %slice.19.x_ref), channel_id=1, source_target_pairs={{0,8},{4,12},{8,16},{12,20},{16,24},{20,28},{24,32},{28,36},{32,40... | collective-permute-start | bytes 1572872 | tf_op jit(solution)/shard_map/ppermute | solution.py:344
  41.1 10.8 %collective-permute-start.3 = (bf16[4,2,128]{2,1,0:T(2,128)(2,1)S(1)}, bf16[4,2,128]{2,1,0:T(2,128)(2,1)S(1)}, u32[]{:S(2)}, u32[]{:S(2)}) collective-permute-start(bf16[4,2,128]{2,1,0:T(2,128)(2,1)S(1)} %get-tuple-element.31), channel_id=1, source_target_pairs={{4,0},{8,4},{12,8},{16,12},{20,16},{24,20},{28,24},{32,28},{36,32}... | collective-permute-start | bytes 6152 | tf_op jit(solution)/shard_map/ppermute | solution.py:344
  45.8 8.3 %collective-permute-start.2 = (bf16[4,2,128]{2,1,0:T(2,128)(2,1)S(1)}, bf16[4,2,128]{2,1,0:T(2,128)(2,1)S(1)}, u32[]{:S(2)}, u32[]{:S(2)}) collective-permute-start(bf16[4,2,128]{2,1,0:T(2,128)(2,1)S(1)} %get-tuple-element.32), channel_id=1, source_target_pairs={{0,4},{4,8},{8,12},{12,16},{16,20},{20,24},{24,28},{28,32},{32,36}... | collective-permute-start | bytes 6152 | tf_op jit(solution)/shard_map/ppermute | solution.py:344
  47.8 0.8 copy-start
  47.8 0.8 copy-start.3
  47.8 0.7 copy-start.1
  47.9 0.7 copy-start.2
  47.9 0.7 copy-start.4
  58.3 3.4 %collective-permute-start.4 = (f32[128,512]{1,0:T(8,128)S(1)}, f32[128,512]{1,0:T(8,128)S(1)}, u32[]{:S(2)}, u32[]{:S(2)}) collective-permute-start(f32[128,512]{1,0:T(8,128)S(1)} %get-tuple-element.22.chosen_ref.own_ref), channel_id=1, source_target_pairs={{0,4},{4,0},{8,12},{12,8},{16,20},{20,16},{24,28},{28,24},{32,36},... | collective-permute-start | bytes 786440 | tf_op jit(solution)/shard_map/ppermute | solution.py:349
  62.1 10.3 %collective-permute-start.5 = (f32[128,512]{1,0:T(8,128)S(1)}, f32[128,512]{1,0:T(8,128)S(1)}, u32[]{:S(2)}, u32[]{:S(2)}) collective-permute-start(f32[128,512]{1,0:T(8,128)S(1)} %pair.1.upper_ref.own_ref), channel_id=1, source_target_pairs={{0,8},{4,12},{8,0},{12,4},{16,24},{20,28},{24,16},{28,20},{32,40},... | collective-permute-start | bytes 786440 | tf_op jit(solution)/shard_map/ppermute | solution.py:349

commit v3 on v2

--- a/solution.py
+++ b/solution.py
@@ -30,6 +30,18 @@
 def column_of(row):
     square = jnp.broadcast_to(row, (128, 128))
     return jnp.sum(jnp.where(iota((128, 128), 0) == iota((128, 128), 1), square, jnp.zeros_like(square)), 1, keepdims=True)
+
+
+def mask(condition):
+    return jnp.where(condition, 1.0, 0.0).astype(BF16)
+
+
+def picked(pick, rows):
+    first = rows.astype(BF16)
+    rest = rows - first.astype(F32)
+    second = rest.astype(BF16)
+    third = (rest - second.astype(F32)).astype(BF16)
+    return dot(pick, first) + dot(pick, second) + dot(pick, third)
 
 
 def side_by_side(ref):
@@ -59,17 +71,18 @@
     within_row = jnp.sum(jnp.where(sub < lane, same, 0.0), 0, keepdims=True)
     within_col = jnp.sum(jnp.where(lane < sub, same, 0.0), 1, keepdims=True)
     slot_row = jnp.where(owner_row >= 0, owner_row * SLOT + within_row, -1.0).astype(jnp.int32)
-    info_row = jnp.where(owner_row >= 0, owner_row * SLOT + CAP, -1.0).astype(jnp.int32)
     lanes = iota((count, 128), 1)
     within_at = within_col.astype(jnp.int32)
     info = jnp.where(lanes == within_at, place_col, 0.0) + jnp.where(lanes == within_at + CAP, label_col, 0.0)
-    table = jnp.concatenate([gen_ref[...], info.astype(BF16)], 0)
+    owns = mask(iota((RANK, count), 0) == owner_row.astype(jnp.int32))
+    table = jnp.concatenate([gen_ref[...], dot(owns, info.astype(BF16)).astype(BF16)], 0)
     rows = out_ref.shape[0]
+    info_row = iota((1, RANK), 1) * SLOT + CAP
+    source_row = jnp.concatenate([slot_row, info_row], 1)
     step = min(256, rows)
     for first in range(0, rows, step):
-        at = iota((step, count), 0) + first
-        pick = jnp.concatenate([jnp.where(at == slot_row, 1.0, 0.0), jnp.where(at == info_row, 1.0, 0.0)], 1)
-        out_ref[first : first + step] = dot(pick.astype(BF16), table).astype(BF16)
+        pick = mask(iota((step, count + RANK), 0) + first == source_row)
+        out_ref[first : first + step] = dot(pick, table).astype(BF16)
 
 
 def route(child_map, child_of, child_gen, devices):
@@ -85,7 +98,7 @@
 
 def one_hot(skel_ref, group, width, shift=0):
     picks = column_of(skel_ref[pl.ds(group, 1), :].astype(F32)).astype(jnp.int32)
-    return jnp.where(iota((RANK, width), 1) == ((picks + shift) & (width - 1)), 1.0, 0.0)
+    return mask(iota((RANK, width), 1) == ((picks + shift) & (width - 1)))
 
 
 def child_kernel(
@@ -116,7 +129,8 @@
     spread = dot(jnp.where(source == iota((count, sources), 1), 1.0, 0.0).astype(BF16), info)
     sub = iota((count, 128), 0)
     slot = sub - SLOT * lax.shift_right_arithmetic(sub * 6554, 16)
-    label = jnp.sum(jnp.where(iota((count, 128), 1) == slot + CAP, spread, 0.0), 1, keepdims=True)
+    ones = jnp.full((128, 128), 1.0, BF16)
+    label = dot(jnp.where(iota((count, 128), 1) == slot + CAP, spread, 0.0).astype(BF16), ones)
     along_t = iota((sources, count), 1)
     source_t = lax.shift_right_arithmetic(along_t * 6554, 16)
     spread_t = dot(info, jnp.where(source_t == iota((sources, count), 0), 1.0, 0.0).astype(BF16), COL_COL)
@@ -125,9 +139,8 @@
     sub_t = iota((128, count), 0)
     code = jnp.sum(jnp.where((sub_t == slot_t) & (sub_t < CAP), spread_t, 0.0), 0, keepdims=True)
     onto = jnp.where(iota((ROWS, count), 0) + 1 == code.astype(jnp.int32), 1.0, 0.0).astype(BF16)
-    wide = got.astype(F32)
-    zero = jnp.zeros_like(wide)
-    parts = jnp.concatenate([jnp.where(label == 0.0, wide, zero), jnp.where(label == 0.0, zero, wide)], 1).astype(BF16)
+    second = got * label.astype(BF16)
+    parts = jnp.concatenate([got - second, second], 1)
     rank = coef_ref.shape[1] // 2
     for s in range(coef_ref.shape[0]):
         coef = coef_ref[s]
@@ -151,9 +164,9 @@
         child_kernel,
         out_shape=[
             jax.ShapeDtypeStruct((coef.shape[0], 2 * ROWS, coef.shape[2]), F32),
-            jax.ShapeDtypeStruct((RANK, 2 * ROWS), F32),
-            jax.ShapeDtypeStruct((RANK, 2 * RANK), F32),
-            jax.ShapeDtypeStruct((RANK, 2 * RANK), F32),
+            jax.ShapeDtypeStruct((RANK, 2 * ROWS), BF16),
+            jax.ShapeDtypeStruct((RANK, 2 * RANK), BF16),
+            jax.ShapeDtypeStruct((RANK, 2 * RANK), BF16),
         ],
         in_specs=[pl.BlockSpec(memory_space=pltpu.SMEM)]
         + [pl.BlockSpec(memory_space=pltpu.VMEM)] * 3
@@ -176,7 +189,7 @@
         leaf_ref[s, 0:8, :] = leaf_ref[s, 0:8, :] - first
         leaf_ref[s, rows - 8 : rows, :] = leaf_ref[s, rows - 8 : rows, :] - last
     own_ref[...] = leaf_ref[where_ref[1]]
-    chosen_ref[...] = dot(pick_ref[...], side_by_side(leaf_ref), precision=HIGHEST)
+    chosen_ref[...] = picked(pick_ref[...], side_by_side(leaf_ref))
 
 
 def leaf(where, part, *others):
@@ -217,7 +230,7 @@
 
 
 def pair_kernel(pick_ref, own_ref, other_ref, out_ref):
-    out_ref[...] = dot(pick_ref[...], jnp.concatenate([own_ref[...], other_ref[...]], 0), precision=HIGHEST)
+    out_ref[...] = picked(pick_ref[...], jnp.concatenate([own_ref[...], other_ref[...]], 0))
 
 
 def pair(pick, own, other):
@@ -231,36 +244,44 @@
     )(pick, own, other)
 
 
-def invert_in_place(refs, width=32):
+def total(terms):
+    while len(terms) > 1:
+        terms = [terms[i] + terms[i + 1] for i in range(0, len(terms), 2)]
+    return terms[0]
+
+
+def eliminated(panel, at, j):
     sub = iota((8, RANK), 0)
     lane = iota((8, RANK), 1)
+    inside = (lane >= at) & (lane < at + 8)
+
+    def along(block, k):
+        return jnp.take_along_axis(block, jnp.full((8, RANK), at + k, jnp.int32), axis=1)
+
+    columns = [along(panel[j], k) for k in range(8)]
+    block = jnp.where(inside, jnp.where(lane - at == sub, 1.0, 0.0), panel[j])
+    for i in range(8):
+        here = sub == i
+        scale = 1.0 / columns[i][i : i + 1, :]
+        factor = jnp.where(here, scale, -columns[i] * scale)
+
+        def reduced(value):
+            return jnp.where(here, 0.0, value) + factor * value[i : i + 1, :]
+
+        block = reduced(block)
+        columns = columns[: i + 1] + [reduced(column) for column in columns[i + 1 :]]
+    return [
+        block
+        if m == j
+        else jnp.where(inside, 0.0, panel[m]) - total([along(panel[m], k) * block[k : k + 1, :] for k in range(8)])
+        for m in range(len(panel))
+    ]
+
+
+def inverses(grams, width):
     wide_lane = iota((width, RANK), 1)
     count, panels = width // 8, RANK // width
-    matrices = [[ref[8 * m : 8 * m + 8, :] for m in range(RANK // 8)] for ref in refs]
-
-    def eliminated(panel, at, j):
-        inside = (lane >= at) & (lane < at + 8)
-
-        def along(block, k):
-            return jnp.take_along_axis(block, jnp.full((8, RANK), at + k, jnp.int32), axis=1)
-
-        columns = [along(panel[j], k) for k in range(8)]
-        block = jnp.where(inside, jnp.where(lane - at == sub, 1.0, 0.0), panel[j])
-        for i in range(8):
-            minus = jnp.where(sub == i, columns[i] - 1.0, columns[i]) * (1.0 / columns[i][i : i + 1, :])
-            block = block - minus * block[i : i + 1, :]
-            for k in range(i + 1, 8):
-                columns[k] = columns[k] - minus * columns[k][i : i + 1, :]
-        result = []
-        for m in range(count):
-            total = block
-            if m != j:
-                total = jnp.where(inside, 0.0, panel[m])
-                for k in range(8):
-                    total = total - along(panel[m], k) * block[k : k + 1, :]
-            result.append(total)
-        return result
-
+    matrices = [[gram[8 * m : 8 * m + 8, :] for m in range(RANK // 8)] for gram in grams]
     for p in range(panels):
         base = p * width
         inside = (wide_lane >= base) & (wide_lane < base + width)
@@ -272,70 +293,121 @@
             for q in [(p + 1 + t) % panels for t in range(panels - 1)]:
                 old = jnp.concatenate(matrix[q * count : (q + 1) * count], 0)
                 new = jnp.where(inside, 0.0, old) - dot(old[:, base : base + width], rows, precision=HIGHEST)
-                for j in range(count):
-                    matrix[q * count + j] = new[8 * j : 8 * j + 8, :]
+                matrix[q * count : (q + 1) * count] = [new[8 * j : 8 * j + 8, :] for j in range(count)]
             matrix[p * count : (p + 1) * count] = panel
-    for ref, matrix in zip(refs, matrices):
-        for m in range(RANK // 8):
-            ref[8 * m : 8 * m + 8, :] = matrix[m]
-
-
-def applied(cross, gram, inverse):
-    unit = jnp.where(iota((RANK, RANK), 0) == iota((RANK, RANK), 1), 1.0, 0.0)
-    rough = dot(cross, inverse, precision=HIGHEST)
-    return rough + dot(rough, unit - dot(gram, inverse, precision=HIGHEST), precision=HIGHEST)
-
-
-def interp_kernel(leaf_gram_ref, leaf_cross_ref, chosen_ref, upper_ref, leaf_out, merge_out, first, second):
+    return [jnp.concatenate(matrix, 0) for matrix in matrices]
+
+
+def invert_between(ref, first, last, width):
+    lane = iota((RANK, RANK), 1)
+    count = width // 8
+
+    def step(p, carry):
+        base = pl.multiple_of(p * width, width)
+        panel = [ref[pl.ds(base + 8 * j, 8), :] for j in range(count)]
+        for j in range(count):
+            panel = eliminated(panel, base + 8 * j, j)
+        whole_matrix = ref[...]
+        left = pltpu.roll(whole_matrix, RANK - base, 1)[:, :width]
+        kept = jnp.where((lane >= base) & (lane < base + width), 0.0, whole_matrix)
+        ref[...] = kept - dot(left, jnp.concatenate(panel, 0), precision=HIGHEST)
+        for j in range(count):
+            ref[pl.ds(base + 8 * j, 8), :] = panel[j]
+        return carry
+
+    lax.fori_loop(first, last, step, 0)
+
+
+def half_rows(where_ref, upper_ref):
+    half = RANK // 2
+    return upper_ref[pl.ds(pl.multiple_of((where_ref[0] & 1) * half, half), half), :]
+
+
+def interp_kernel(
+    where_ref, leaf_gram_ref, leaf_cross_ref, chosen_ref, upper_ref, pick_ref,
+    leaf_out, merge_out, mine_out, inverse_out, part_out, count_out,
+):
     upper = upper_ref[...]
-    merge_gram = dot(upper, upper, ROW_ROW, HIGHEST)
-    first[...] = leaf_gram_ref[...]
-    second[...] = merge_gram
-    invert_in_place([first, second])
+    pick = pick_ref[:, :RANK]
+    mine = picked(pick, upper)
+    mine_out[...] = mine
+    taken = jnp.sum(pick.astype(F32), 1, keepdims=True)
+    count_out[0] = jnp.sum(taken).astype(jnp.int32)
+    diagonal = iota((RANK, RANK), 0) == iota((RANK, RANK), 1)
+    others = jnp.where(diagonal, 1.0 - taken, 0.0)
+    leaf_inverse, merge_inverse, mine_inverse = inverses(
+        [leaf_gram_ref[...], dot(upper, upper, ROW_ROW, HIGHEST), dot(mine, mine, ROW_ROW, HIGHEST) + others], 32
+    )
+    inverse_out[...] = mine_inverse - others
     merge_cross = dot(chosen_ref[...], upper, ROW_ROW, HIGHEST)
-    leaf_out[...] = applied(leaf_cross_ref[...], leaf_gram_ref[...], first[...])
-    merge_out[...] = applied(merge_cross, merge_gram, second[...])
-
-
-def interp(leaf_gram, leaf_cross, chosen, upper):
+    half = half_rows(where_ref, upper_ref)
+    part_out[...] = dot(dot(half, mine, ROW_ROW, HIGHEST), mine_inverse - others, precision=HIGHEST)
+    leaf_out[...] = dot(leaf_cross_ref[...], leaf_inverse, precision=HIGHEST)
+    merge_out[...] = dot(merge_cross, merge_inverse, precision=HIGHEST)
+
+
+def interp(where, leaf_gram, leaf_cross, chosen, upper, pick):
     return pl.pallas_call(
         interp_kernel,
         out_shape=[
             jax.ShapeDtypeStruct(leaf_cross.shape, F32),
             jax.ShapeDtypeStruct((RANK, RANK), F32),
+            jax.ShapeDtypeStruct(upper.shape, F32),
+            jax.ShapeDtypeStruct((RANK, RANK), F32),
+            jax.ShapeDtypeStruct((RANK // 2, RANK), F32),
+            jax.ShapeDtypeStruct((1,), jnp.int32),
         ],
-        in_specs=[pl.BlockSpec(memory_space=pltpu.VMEM)] * 4,
-        out_specs=[pl.BlockSpec(memory_space=pltpu.VMEM)] * 2,
-        scratch_shapes=[pltpu.VMEM((RANK, RANK), F32)] * 2,
+        in_specs=[pl.BlockSpec(memory_space=pltpu.SMEM)] + [pl.BlockSpec(memory_space=pltpu.VMEM)] * 5,
+        out_specs=[pl.BlockSpec(memory_space=pltpu.VMEM)] * 5 + [pl.BlockSpec(memory_space=pltpu.SMEM)],
         cost_estimate=pl.CostEstimate(flops=8_000_000_000, bytes_accessed=2_000_000, transcendentals=0),
         compiler_params=pltpu.CompilerParams(vmem_limit_bytes=VMEM_LIMIT),
         name="interp",
-    )(leaf_gram, leaf_cross, chosen, upper)
-
-
-def top_kernel(where_ref, pick_ref, own_ref, other_ref, top_out, rows_out, gram, quad):
-    position = where_ref[0]
-    chosen = dot(pick_ref[...], jnp.concatenate([own_ref[...], other_ref[...]], 0), precision=HIGHEST)
-    quad[...] = chosen
-    top_gram = dot(chosen, chosen, ROW_ROW, HIGHEST)
-    gram[...] = top_gram
+    )(where, leaf_gram, leaf_cross, chosen, upper, pick)
+
+
+def top_kernel(
+    where_ref, count_ref, pick_ref, upper_ref, across_ref, mine_ref, inverse_ref, part_ref,
+    top_out, rows_out, rest, quad,
+):
+    position, width = where_ref[0], 16
+    pick = pick_ref[:, RANK:]
+    theirs = picked(pick, across_ref[...])
+    mine, inverse, part = mine_ref[...], inverse_ref[...], part_ref[...]
+    quad[...] = mine + theirs
     columns = pl.ds(pl.multiple_of(where_ref[1] * 128, 128), 128)
     rows_out[...] = quad[pl.ds(pl.multiple_of((position & 3) * (RANK // 4), RANK // 4), RANK // 4), columns]
-    invert_in_place([gram], 64)
-    own = own_ref[pl.ds(pl.multiple_of((position & 1) * (RANK // 2), RANK // 2), RANK // 2), :]
-    top_out[...] = applied(dot(own, chosen, ROW_ROW, HIGHEST), top_gram, gram[...])
-
-
-def top(where, pick, own, other):
+    mixed = dot(mine, theirs, ROW_ROW, HIGHEST)
+    passed = dot(inverse, mixed, precision=HIGHEST)
+    taken = jnp.sum(pick.astype(F32), 1, keepdims=True)
+    diagonal = iota((RANK, RANK), 0) == iota((RANK, RANK), 1)
+    rest[...] = (
+        dot(theirs, theirs, ROW_ROW, HIGHEST)
+        - dot(mixed, passed, COL_COL, HIGHEST)
+        + jnp.where(diagonal, 1.0 - taken, 0.0)
+    )
+    half = half_rows(where_ref, upper_ref)
+    cross = dot(half, theirs, ROW_ROW, HIGHEST) - dot(part, mixed, precision=HIGHEST)
+    own_count = count_ref[0]
+    own_first = (lax.shift_right_arithmetic(position, 1) & 1) == 0
+    begin = jnp.where(own_first, own_count, 0)
+    end = jnp.where(own_first, RANK, RANK - own_count)
+    invert_between(
+        rest, lax.shift_right_arithmetic(begin, 4), lax.shift_right_arithmetic(end + width - 1, 4), width
+    )
+    side = dot(cross, rest[...], precision=HIGHEST)
+    top_out[...] = part + side - dot(side, passed, ROW_ROW, HIGHEST)
+
+
+def top(where, count, pick, upper, across, mine, inverse, part):
     return pl.pallas_call(
         top_kernel,
         out_shape=[jax.ShapeDtypeStruct((RANK // 2, RANK), F32), jax.ShapeDtypeStruct((RANK // 4, 128), F32)],
-        in_specs=[pl.BlockSpec(memory_space=pltpu.SMEM)] + [pl.BlockSpec(memory_space=pltpu.VMEM)] * 3,
+        in_specs=[pl.BlockSpec(memory_space=pltpu.SMEM)] * 2 + [pl.BlockSpec(memory_space=pltpu.VMEM)] * 6,
         out_specs=[pl.BlockSpec(memory_space=pltpu.VMEM)] * 2,
-        scratch_shapes=[pltpu.VMEM((RANK, RANK), F32), pltpu.VMEM(own.shape, F32)],
+        scratch_shapes=[pltpu.VMEM((RANK, RANK), F32), pltpu.VMEM(upper.shape, F32)],
         compiler_params=pltpu.CompilerParams(vmem_limit_bytes=VMEM_LIMIT),
         name="top",
-    )(where, pick, own, other)
+    )(where, count, pick, upper, across, mine, inverse, part)
 
 
 def shifted(value, axis, steps):
@@ -368,15 +440,17 @@
     high = shifted(wide, "row", -offset)
     left = shifted(wide[:, -2:], "row", 1)
     right = shifted(wide[:, :2], "row", -1)
-    part, leaf_pick, pair_pick, quad_pick = child(
+    base, leaf_pick, pair_pick, quad_pick = child(
         where, got, coef, wide, shift_real.reshape(-1, 128), shift_imag.reshape(-1, 128),
         leaf_skel, pair_skel, quad_skel,
     )
-    own, leaf_rows, chosen = leaf(where, part, low, high, left, right, leaf_pick)
+    own, leaf_rows, chosen = leaf(where, base, low, high, left, right, leaf_pick)
     leaf_gram, leaf_cross = products(leaf_rows, chosen)
     upper = pair(pair_pick, chosen, swapped(chosen, "row", 0))
-    leaf_interp, merge_interp = interp(leaf_gram, leaf_cross, chosen, upper)
-    top_interp, top_rows = top(where, quad_pick, upper, swapped(upper, "row", 1))
+    leaf_interp, merge_interp, mine, inverse, part, count = interp(
+        where, leaf_gram, leaf_cross, chosen, upper, quad_pick
+    )
+    top_interp, top_rows = top(where, count, quad_pick, upper, swapped(upper, "row", 1), mine, inverse, part)
     return own.reshape(row_count, 2, col_count), leaf_interp, merge_interp, top_interp, top_rows
 
 

time: 80 us -> 79.3 us (level)
  the two profiles are of different devices: /device:TPU:32 before, /device:TPU:33 now
where the time goes in v3:
time: 79.3 us; the launch traced here: 78.9 us
  starting transfers between devices  38 us (48%)
  Pallas kernels  24.2 us (31%)
  blocking collectives  11.7 us (15%)
  waiting for transfers between devices  3.29 us (4%)
  between operations  0.84 us (1%)
    all_to_all x1, starting transfers between devices, body(): lax.all_to_all(outgoing.reshape(devices * SLOT // 2, 2, -1), 'row', split...  17.8 us
    ppermute x4, starting transfers between devices, shifted(): lax.ppermute(value, axis, [(source, source + steps) for source in range(f...  12.9 us
    all_gather x1, blocking collectives, body(): lax.all_gather(jnp.concatenate([probe.reshape(-1, col_count), child_coef....  11.7 us
    pallas_call x1, Pallas kernels, interp(): pl.pallas_call(interp_kernel, out_shape=[jax.ShapeDtypeStruct(leaf_cross....  8.24 us
    ppermute x2, starting transfers between devices, swapped(): lax.ppermute(block, axis, [(i, i ^ 1 << apart) for i in range(count)])  7.33 us
    pallas_call x1, Pallas kernels, top(): pl.pallas_call(top_kernel, out_shape=[jax.ShapeDtypeStruct((RANK // 2, RA...  6.38 us
    pallas_call x1, Pallas kernels, child(): pl.pallas_call(child_kernel, out_shape=[jax.ShapeDtypeStruct((coef.shape[...  3.49 us
    ppermute x4, waiting for transfers between devices, shifted(): lax.ppermute(value, axis, [(source, source + steps) for source in range(f...  3.28 us
  transfers between devices with their start and end apart: 7, of which 1 were waited for; matrix products, arithmetic and copies ran while one was open for 0% of the time, Pallas kernels for 16%

profile of v3, /device:TPU:33, one launch (start us, length us, event | category | flops | bytes accessed | tf_op | source)
XLA Modules:
  0.0 78.9 jit_solution(17772420643968405524)
XLA Ops:
  0.6 2.9 %route.1 = bf16[1280,128]{1,0:T(8,128)(2,1)} custom-call(s32[4]{0:T(128)} %of_ref.1, s32[4,128]{1,0:T(4,128)} %map_ref.1, bf16[512,128]{1,0:T(8,128)(2,1)} %gen_ref.1), custom_call_target="tpu_custom_call" | custom-call | tf_op jit(solution)/shard_map/route/pallas_call | solution.py:89
  3.5 17.8 %all-to-all-start = ((bf16[640,2,128]{2,1,0:T(2,128)(2,1)}), bf16[640,2,128]{2,1,0:T(2,128)(2,1)S(1)}, u32[]{:S(2)}, u32[]{:S(2)}) async-start(bf16[640,2,128]{2,1,0:T(2,128)(2,1)} %bitcast.16), calls=%async_computation | async-start | bytes 655360 | tf_op jit(solution)/shard_map/all_to_all | solution.py:436
  21.3 0.0 copy-done.5
  21.3 0.0 copy-done.6
  21.3 11.7 %all-gather = bf16[2560,128]{1,0:T(8,128)(2,1)S(1)} all-gather(bf16[640,128]{1,0:T(8,128)(2,1)S(1)} %pad_maximum_fusion), channel_id=2, replica_groups=mesh['row'=128,'samp'=4] {'samp'}, dimensions={0}, use_global_device_ids=true | all-gather | bytes 819200 | tf_op jit(solution)/shard_map/all_gather | solution.py:431
  33.1 4.3 %collective-permute-start.1 = (bf16[4,512,128]{2,1,0:T(8,128)(2,1)S(1)}, bf16[4,512,128]{2,1,0:T(8,128)(2,1)S(1)}, u32[]{:S(2)}, u32[]{:S(2)}) collective-permute-start(bf16[4,512,128]{2,1,0:T(8,128)(2,1)S(1)} %slice.19.x_ref), channel_id=1, source_target_pairs={{8,0},{12,4},{16,8},{20,12},{24,16},{28,20},{32,24},{36,28},{40,32... | collective-permute-start | bytes 1572872 | tf_op jit(solution)/shard_map/ppermute | solution.py:416
  37.4 1.9 %collective-permute-start = (bf16[4,512,128]{2,1,0:T(8,128)(2,1)S(1)}, bf16[4,512,128]{2,1,0:T(8,128)(2,1)S(1)}, u32[]{:S(2)}, u32[]{:S(2)}) collective-permute-start(bf16[4,512,128]{2,1,0:T(8,128)(2,1)S(1)} %slice.19.x_ref), channel_id=1, source_target_pairs={{0,8},{4,12},{8,16},{12,20},{16,24},{20,28},{24,32},{28,36},{32,40... | collective-permute-start | bytes 1572872 | tf_op jit(solution)/shard_map/ppermute | solution.py:416
  39.3 4.3 %collective-permute-start.3 = (bf16[4,2,128]{2,1,0:T(2,128)(2,1)S(1)}, bf16[4,2,128]{2,1,0:T(2,128)(2,1)S(1)}, u32[]{:S(2)}, u32[]{:S(2)}) collective-permute-start(bf16[4,2,128]{2,1,0:T(2,128)(2,1)S(1)} %get-tuple-element.39), channel_id=1, source_target_pairs={{4,0},{8,4},{12,8},{16,12},{20,16},{24,20},{28,24},{32,28},{36,32}... | collective-permute-start | bytes 6152 | tf_op jit(solution)/shard_map/ppermute | solution.py:416
  43.6 2.4 %collective-permute-start.2 = (bf16[4,2,128]{2,1,0:T(2,128)(2,1)S(1)}, bf16[4,2,128]{2,1,0:T(2,128)(2,1)S(1)}, u32[]{:S(2)}, u32[]{:S(2)}) collective-permute-start(bf16[4,2,128]{2,1,0:T(2,128)(2,1)S(1)} %get-tuple-element.40), channel_id=1, source_target_pairs={{0,4},{4,8},{8,12},{12,16},{16,20},{20,24},{24,28},{28,32},{32,36}... | collective-permute-start | bytes 6152 | tf_op jit(solution)/shard_map/ppermute | solution.py:416
  46.0 0.0 copy-start
  46.0 0.0 copy-start.3
  46.0 0.0 copy-start.1
  46.1 0.1 pad_add_fusion.where_ref
  46.1 0.0 all-to-all-done
  46.1 0.6 copy-done
  46.8 0.0 copy-done.1
  46.8 0.1 copy-done.2
  46.8 0.0 copy-done.4
  46.8 3.5 %child.1 = (f32[4,512,128]{2,1,0:T(8,128)S(1)}, bf16[128,512]{1,0:T(8,128)(2,1)S(1)}, bf16[128,256]{1,0:T(8,128)(2,1)S(1)}, bf16[128,256]{1,0:T(8,128)(2,1)S(1)}) custom-call(s32[2]{0:T(128)S(1)} %pad_add_fusion.where_ref, bf16[1280,128]{1,0:T(8,128)(2,1)S(1)} %bitcast.10, bf16[4,128,128]{2,1,0:T(8,128)(2,1)S(1)} %slice.18.coef_ref, ...), custom_call_target="tpu_custom_call" | custom-call | flops 2000000000 | bytes 2000000 | tf_op jit(solution)/shard_map/child/pallas_call | solution.py:163
  50.3 0.0 collective-permute-done.3.right_ref
  50.3 0.0 collective-permute-done.2.left_ref
  50.4 0.0 collective-permute-done.1.high_ref
  50.4 3.3 %collective-permute-done.low_ref = bf16[4,512,128]{2,1,0:T(8,128)(2,1)S(1)} collective-permute-done((bf16[4,512,128]{2,1,0:T(8,128)(2,1)S(1)}, bf16[4,512,128]{2,1,0:T(8,128)(2,1)S(1)}, u32[]{:S(2)}, u32[]{:S(2)}) %collective-permute-start) | collective-permute-done | bytes 524320 | tf_op jit(solution)/shard_map/ppermute | solution.py:416
  53.6 1.7 %leaf.1 = (f32[512,128]{1,0:T(8,128)}, f32[4,512,128]{2,1,0:T(8,128)S(1)}, f32[128,512]{1,0:T(8,128)S(1)}) custom-call(s32[2]{0:T(128)S(1)} %pad_add_fusion.where_ref, f32[4,512,128]{2,1,0:T(8,128)S(1)} %get-tuple-element.22.part_ref, bf16[4,512,128]{2,1,0:T(8,128)(2,1)S(1)} %collective-permute-done.low_ref, ...), custom_call_target="tpu_custom_call" | custom-call | tf_op jit(solution)/shard_map/leaf/pallas_call | solution.py:197
  55.4 5.2 %collective-permute-start.4 = (f32[128,512]{1,0:T(8,128)S(1)}, f32[128,512]{1,0:T(8,128)S(1)}, u32[]{:S(2)}, u32[]{:S(2)}) collective-permute-start(f32[128,512]{1,0:T(8,128)S(1)} %get-tuple-element.26.chosen_ref.own_ref), channel_id=1, source_target_pairs={{0,4},{4,0},{8,12},{12,8},{16,20},{20,16},{24,28},{28,24},{32,36},... | collective-permute-start | bytes 786440 | tf_op jit(solution)/shard_map/ppermute | solution.py:421
  60.6 1.2 %products.1 = (f32[128,128]{1,0:T(8,128)S(1)}, f32[512,128]{1,0:T(8,128)S(1)}) custom-call(f32[4,512,128]{2,1,0:T(8,128)S(1)} %get-tuple-element.25.leaf_ref, f32[128,512]{1,0:T(8,128)S(1)} %get-tuple-element.26.chosen_ref.own_ref), custom_call_target="tpu_custom_call" | custom-call | flops 1000000000 | bytes 2000000 | tf_op jit(solution)/shard_map/products/pallas_call | solution.py:218
  61.8 0.0 collective-permute-done.4.other_ref
  61.8 0.3 pair.1.upper_ref
  62.1 2.1 %collective-permute-start.5 = (f32[128,512]{1,0:T(8,128)S(1)}, f32[128,512]{1,0:T(8,128)S(1)}, u32[]{:S(2)}, u32[]{:S(2)}) collective-permute-start(f32[128,512]{1,0:T(8,128)S(1)} %pair.1.upper_ref), channel_id=1, source_target_pairs={{0,8},{4,12},{8,0},{12,4},{16,24},{20,28},{24,16},{28,20},{32,40},... | collective-permute-start | bytes 786440 | tf_op jit(solution)/shard_map/ppermute | solution.py:421
  64.3 8.2 %interp.1 = (f32[512,128]{1,0:T(8,128)}, f32[128,128]{1,0:T(8,128)}, f32[128,512]{1,0:T(8,128)S(1)}, f32[128,128]{1,0:T(8,128)S(1)}, f32[64,128]{1,0:T(8,128)S(1)}, /*index=5*/s32[1]{0:T(128)}) custom-call(s32[2]{0:T(128)S(1)} %pad_add_fusion.where_ref, f32[128,128]{1,0:T(8,128)S(1)} %get-tuple-element.27.leaf_gram_ref, ...), custom_call_target="tpu_custom_call" | custom-call | flops 8000000000 | bytes 2000000 | tf_op jit(solution)/shard_map/interp/pallas_call | solution.py:350
  72.5 0.0 collective-permute-done.5.across_ref
  72.5 6.4 %top.1 = (f32[64,128]{1,0:T(8,128)}, f32[32,128]{1,0:T(8,128)}) custom-call(s32[2]{0:T(128)S(1)} %pad_add_fusion.where_ref, s32[1]{0:T(128)} %get-tuple-element.33.count_ref, bf16[128,256]{1,0:T(8,128)(2,1)S(1)} %get-tuple-element.30.pick_ref, f32[128,512]{1,0:T(8,128)S(1)} %pair.1.upper_ref, f32[128,512]{1,0:T(8,128)S(1)} %collective-permute-done.5.across_ref, ...), custom_call_target="tpu_custom_call" | custom-call | tf_op jit(solution)/shard_map/top/pallas_call | solution.py:402
  (9 shorter events, 0.1 us)
Async XLA Ops:
  3.5 17.8 %copy-start.5 = (bf16[256,2,128]{2,1,0:T(2,128)(2,1)S(1)}, bf16[256,2,128]{2,1,0:T(2,128)(2,1)}, u32[]{:S(2)}) copy-start(bf16[256,2,128]{2,1,0:T(2,128)(2,1)} %param.10) | copy-start | bytes 393220
  3.5 17.8 %copy-start.6 = (bf16[2,64,128]{2,1,0:T(8,128)(2,1)S(1)}, bf16[2,64,128]{2,1,0:T(8,128)(2,1)}, u32[]{:S(2)}) copy-start(bf16[2,64,128]{2,1,0:T(8,128)(2,1)} %param.14) | copy-start | bytes 98308
  3.5 42.6 %all-to-all-start = ((bf16[640,2,128]{2,1,0:T(2,128)(2,1)}), bf16[640,2,128]{2,1,0:T(2,128)(2,1)S(1)}, u32[]{:S(2)}, u32[]{:S(2)}) async-start(bf16[640,2,128]{2,1,0:T(2,128)(2,1)} %bitcast.16), calls=%async_computation | async-start | bytes 655360 | tf_op jit(solution)/shard_map/all_to_all | solution.py:436
  33.1 17.3 %collective-permute-start.1 = (bf16[4,512,128]{2,1,0:T(8,128)(2,1)S(1)}, bf16[4,512,128]{2,1,0:T(8,128)(2,1)S(1)}, u32[]{:S(2)}, u32[]{:S(2)}) collective-permute-start(bf16[4,512,128]{2,1,0:T(8,128)(2,1)S(1)} %slice.19.x_ref), channel_id=1, source_target_pairs={{8,0},{12,4},{16,8},{20,12},{24,16},{28,20},{32,24},{36,28},{40,32... | collective-permute-start | bytes 1572872 | tf_op jit(solution)/shard_map/ppermute | solution.py:416
  37.4 16.2 %collective-permute-start = (bf16[4,512,128]{2,1,0:T(8,128)(2,1)S(1)}, bf16[4,512,128]{2,1,0:T(8,128)(2,1)S(1)}, u32[]{:S(2)}, u32[]{:S(2)}) collective-permute-start(bf16[4,512,128]{2,1,0:T(8,128)(2,1)S(1)} %slice.19.x_ref), channel_id=1, source_target_pairs={{0,8},{4,12},{8,16},{12,20},{16,24},{20,28},{24,32},{28,36},{32,40... | collective-permute-start | bytes 1572872 | tf_op jit(solution)/shard_map/ppermute | solution.py:416
  39.3 11.0 %collective-permute-start.3 = (bf16[4,2,128]{2,1,0:T(2,128)(2,1)S(1)}, bf16[4,2,128]{2,1,0:T(2,128)(2,1)S(1)}, u32[]{:S(2)}, u32[]{:S(2)}) collective-permute-start(bf16[4,2,128]{2,1,0:T(2,128)(2,1)S(1)} %get-tuple-element.39), channel_id=1, source_target_pairs={{4,0},{8,4},{12,8},{16,12},{20,16},{24,20},{28,24},{32,28},{36,32}... | collective-permute-start | bytes 6152 | tf_op jit(solution)/shard_map/ppermute | solution.py:416
  43.6 6.7 %collective-permute-start.2 = (bf16[4,2,128]{2,1,0:T(2,128)(2,1)S(1)}, bf16[4,2,128]{2,1,0:T(2,128)(2,1)S(1)}, u32[]{:S(2)}, u32[]{:S(2)}) collective-permute-start(bf16[4,2,128]{2,1,0:T(2,128)(2,1)S(1)} %get-tuple-element.40), channel_id=1, source_target_pairs={{0,4},{4,8},{8,12},{12,16},{16,20},{20,24},{24,28},{28,32},{32,36}... | collective-permute-start | bytes 6152 | tf_op jit(solution)/shard_map/ppermute | solution.py:416
  46.0 0.8 copy-start
  46.0 0.8 copy-start.3
  46.0 0.7 copy-start.1
  46.1 0.7 copy-start.2
  46.1 0.7 copy-start.4
  55.4 6.4 %collective-permute-start.4 = (f32[128,512]{1,0:T(8,128)S(1)}, f32[128,512]{1,0:T(8,128)S(1)}, u32[]{:S(2)}, u32[]{:S(2)}) collective-permute-start(f32[128,512]{1,0:T(8,128)S(1)} %get-tuple-element.26.chosen_ref.own_ref), channel_id=1, source_target_pairs={{0,4},{4,0},{8,12},{12,8},{16,20},{20,16},{24,28},{28,24},{32,36},... | collective-permute-start | bytes 786440 | tf_op jit(solution)/shard_map/ppermute | solution.py:421
  62.1 10.4 %collective-permute-start.5 = (f32[128,512]{1,0:T(8,128)S(1)}, f32[128,512]{1,0:T(8,128)S(1)}, u32[]{:S(2)}, u32[]{:S(2)}) collective-permute-start(f32[128,512]{1,0:T(8,128)S(1)} %pair.1.upper_ref), channel_id=1, source_target_pairs={{0,8},{4,12},{8,0},{12,4},{16,24},{20,28},{24,16},{28,20},{32,40},... | collective-permute-start | bytes 786440 | tf_op jit(solution)/shard_map/ppermute | solution.py:421

commit v4 on v3

--- a/solution.py
+++ b/solution.py
@@ -421,6 +421,12 @@
     return lax.ppermute(block, axis, [(i, i ^ (1 << apart)) for i in range(count)])
 
 
+def crossed(block, axis, width):
+    count = lax.axis_size(axis)
+    up = [(i, i + width) for i in range(count - width) if i // width % 2 == 1]
+    return lax.ppermute(block, axis, up + [(high, low) for low, high in up])
+
+
 def body(
     probe, shift_real, shift_imag, child_gen, child_coef, child_map, child_of, leaf_skel, pair_skel, quad_skel
 ):
@@ -436,8 +442,8 @@
     got = lax.all_to_all(
         outgoing.reshape(devices * SLOT // 2, 2, -1), "row", split_axis=0, concat_axis=0, tiled=True
     ).reshape(devices * SLOT, -1)
-    low = shifted(wide, "row", offset)
-    high = shifted(wide, "row", -offset)
+    high = crossed(wide, "row", offset)
+    low = swapped(wide, "row", 1)
     left = shifted(wide[:, -2:], "row", 1)
     right = shifted(wide[:, :2], "row", -1)
     base, leaf_pick, pair_pick, quad_pick = child(

time: 79.3 us -> 76.7 us (0.967)
  the two profiles are of different devices: /device:TPU:33 before, /device:TPU:1 now
where the time goes in v4:
time: 76.7 us; the launch traced here: 76.3 us
  starting transfers between devices  37.1 us (48%)
  Pallas kernels  23.7 us (31%)
  blocking collectives  12.2 us (16%)
  waiting for transfers between devices  1.63 us (2%)
  between operations  0.82 us (1%)
    all_to_all x1, starting transfers between devices, body(): lax.all_to_all(outgoing.reshape(devices * SLOT // 2, 2, -1), 'row', split...  18.5 us
    all_gather x1, blocking collectives, body(): lax.all_gather(jnp.concatenate([probe.reshape(-1, col_count), child_coef....  12.2 us
    ppermute x3, starting transfers between devices, swapped(): lax.ppermute(block, axis, [(i, i ^ 1 << apart) for i in range(count)])  11.4 us
    pallas_call x1, Pallas kernels, interp(): pl.pallas_call(interp_kernel, out_shape=[jax.ShapeDtypeStruct(leaf_cross....  8.24 us
    ppermute x2, starting transfers between devices, shifted(): lax.ppermute(value, axis, [(source, source + steps) for source in range(f...  6.49 us
    pallas_call x1, Pallas kernels, top(): pl.pallas_call(top_kernel, out_shape=[jax.ShapeDtypeStruct((RANK // 2, RA...  5.86 us
    pallas_call x1, Pallas kernels, child(): pl.pallas_call(child_kernel, out_shape=[jax.ShapeDtypeStruct((coef.shape[...  3.49 us
    pallas_call x1, Pallas kernels, route(): pl.pallas_call(route_kernel, out_shape=jax.ShapeDtypeStruct((devices * SL...  2.88 us
  transfers between devices with their start and end apart: 7, of which 1 were waited for; matrix products, arithmetic and copies ran while one was open for 0% of the time, Pallas kernels for 17%

profile of v4, /device:TPU:1, one launch (start us, length us, event | category | flops | bytes accessed | tf_op | source)
XLA Modules:
  0.0 76.3 jit_solution(7557131362216056964)
XLA Ops:
  0.6 2.9 %route.1 = bf16[1280,128]{1,0:T(8,128)(2,1)} custom-call(s32[4]{0:T(128)} %of_ref.1, s32[4,128]{1,0:T(4,128)} %map_ref.1, bf16[512,128]{1,0:T(8,128)(2,1)} %gen_ref.1), custom_call_target="tpu_custom_call" | custom-call | tf_op jit(solution)/shard_map/route/pallas_call | solution.py:89
  3.5 18.5 %all-to-all-start = ((bf16[640,2,128]{2,1,0:T(2,128)(2,1)}), bf16[640,2,128]{2,1,0:T(2,128)(2,1)S(1)}, u32[]{:S(2)}, u32[]{:S(2)}) async-start(bf16[640,2,128]{2,1,0:T(2,128)(2,1)} %bitcast.16), calls=%async_computation | async-start | bytes 655360 | tf_op jit(solution)/shard_map/all_to_all | solution.py:442
  22.1 0.0 copy-done.5
  22.1 0.0 copy-done.6
  22.1 12.2 %all-gather = bf16[2560,128]{1,0:T(8,128)(2,1)S(1)} all-gather(bf16[640,128]{1,0:T(8,128)(2,1)S(1)} %pad_maximum_fusion), channel_id=2, replica_groups=mesh['row'=128,'samp'=4] {'samp'}, dimensions={0}, use_global_device_ids=true | all-gather | bytes 819200 | tf_op jit(solution)/shard_map/all_gather | solution.py:437
  34.3 0.7 collective-permute-start.1
  35.0 5.2 %collective-permute-start = (bf16[4,512,128]{2,1,0:T(8,128)(2,1)S(1)}, bf16[4,512,128]{2,1,0:T(8,128)(2,1)S(1)}, u32[]{:S(2)}, u32[]{:S(2)}) collective-permute-start(bf16[4,512,128]{2,1,0:T(8,128)(2,1)S(1)} %slice.19.x_ref), channel_id=1, source_target_pairs={{0,8},{4,12},{8,0},{12,4},{16,24},{20,28},{24,16},{28,20},{32,40},... | collective-permute-start | bytes 1572872 | tf_op jit(solution)/shard_map/ppermute | solution.py:421
  40.3 4.6 %collective-permute-start.3 = (bf16[4,2,128]{2,1,0:T(2,128)(2,1)S(1)}, bf16[4,2,128]{2,1,0:T(2,128)(2,1)S(1)}, u32[]{:S(2)}, u32[]{:S(2)}) collective-permute-start(bf16[4,2,128]{2,1,0:T(2,128)(2,1)S(1)} %get-tuple-element.39), channel_id=1, source_target_pairs={{4,0},{8,4},{12,8},{16,12},{20,16},{24,20},{28,24},{32,28},{36,32}... | collective-permute-start | bytes 6152 | tf_op jit(solution)/shard_map/ppermute | solution.py:416
  44.9 1.9 %collective-permute-start.2 = (bf16[4,2,128]{2,1,0:T(2,128)(2,1)S(1)}, bf16[4,2,128]{2,1,0:T(2,128)(2,1)S(1)}, u32[]{:S(2)}, u32[]{:S(2)}) collective-permute-start(bf16[4,2,128]{2,1,0:T(2,128)(2,1)S(1)} %get-tuple-element.40), channel_id=1, source_target_pairs={{0,4},{4,8},{8,12},{12,16},{16,20},{20,24},{24,28},{28,32},{32,36}... | collective-permute-start | bytes 6152 | tf_op jit(solution)/shard_map/ppermute | solution.py:416
  46.8 0.0 copy-start
  46.8 0.0 copy-start.3
  46.8 0.0 copy-start.1
  46.9 0.1 pad_add_fusion.where_ref
  46.9 0.0 all-to-all-done
  46.9 0.6 copy-done
  47.6 0.0 copy-done.3
  47.6 0.0 copy-done.1
  47.6 0.1 copy-done.2
  47.6 3.5 %child.1 = (f32[4,512,128]{2,1,0:T(8,128)S(1)}, bf16[128,512]{1,0:T(8,128)(2,1)S(1)}, bf16[128,256]{1,0:T(8,128)(2,1)S(1)}, bf16[128,256]{1,0:T(8,128)(2,1)S(1)}) custom-call(s32[2]{0:T(128)S(1)} %pad_add_fusion.where_ref, bf16[1280,128]{1,0:T(8,128)(2,1)S(1)} %bitcast.10, bf16[4,128,128]{2,1,0:T(8,128)(2,1)S(1)} %slice.18.coef_ref, ...), custom_call_target="tpu_custom_call" | custom-call | flops 2000000000 | bytes 2000000 | tf_op jit(solution)/shard_map/child/pallas_call | solution.py:163
  51.1 1.6 %collective-permute-done.3.right_ref = bf16[4,2,128]{2,1,0:T(2,128)(2,1)S(1)} collective-permute-done((bf16[4,2,128]{2,1,0:T(2,128)(2,1)S(1)}, bf16[4,2,128]{2,1,0:T(2,128)(2,1)S(1)}, u32[]{:S(2)}, u32[]{:S(2)}) %collective-permute-start.3) | collective-permute-done | bytes 2080 | tf_op jit(solution)/shard_map/ppermute | solution.py:416
  52.7 0.0 collective-permute-done.2.left_ref
  52.7 0.0 collective-permute-done.1.high_ref
  52.7 0.0 collective-permute-done.low_ref
  52.7 1.7 %leaf.1 = (f32[512,128]{1,0:T(8,128)}, f32[4,512,128]{2,1,0:T(8,128)S(1)}, f32[128,512]{1,0:T(8,128)S(1)}) custom-call(s32[2]{0:T(128)S(1)} %pad_add_fusion.where_ref, f32[4,512,128]{2,1,0:T(8,128)S(1)} %get-tuple-element.22.part_ref, bf16[4,512,128]{2,1,0:T(8,128)(2,1)S(1)} %collective-permute-done.low_ref, ...), custom_call_target="tpu_custom_call" | custom-call | tf_op jit(solution)/shard_map/leaf/pallas_call | solution.py:197
  54.5 2.3 %collective-permute-start.4 = (f32[128,512]{1,0:T(8,128)S(1)}, f32[128,512]{1,0:T(8,128)S(1)}, u32[]{:S(2)}, u32[]{:S(2)}) collective-permute-start(f32[128,512]{1,0:T(8,128)S(1)} %get-tuple-element.26.chosen_ref.own_ref), channel_id=1, source_target_pairs={{0,4},{4,0},{8,12},{12,8},{16,20},{20,16},{24,28},{28,24},{32,36},... | collective-permute-start | bytes 786440 | tf_op jit(solution)/shard_map/ppermute | solution.py:421
  56.8 1.2 %products.1 = (f32[128,128]{1,0:T(8,128)S(1)}, f32[512,128]{1,0:T(8,128)S(1)}) custom-call(f32[4,512,128]{2,1,0:T(8,128)S(1)} %get-tuple-element.25.leaf_ref, f32[128,512]{1,0:T(8,128)S(1)} %get-tuple-element.26.chosen_ref.own_ref), custom_call_target="tpu_custom_call" | custom-call | flops 1000000000 | bytes 2000000 | tf_op jit(solution)/shard_map/products/pallas_call | solution.py:218
  58.0 0.0 collective-permute-done.4.other_ref
  58.0 0.3 pair.1.upper_ref
  58.3 3.9 %collective-permute-start.5 = (f32[128,512]{1,0:T(8,128)S(1)}, f32[128,512]{1,0:T(8,128)S(1)}, u32[]{:S(2)}, u32[]{:S(2)}) collective-permute-start(f32[128,512]{1,0:T(8,128)S(1)} %pair.1.upper_ref), channel_id=1, source_target_pairs={{0,8},{4,12},{8,0},{12,4},{16,24},{20,28},{24,16},{28,20},{32,40},... | collective-permute-start | bytes 786440 | tf_op jit(solution)/shard_map/ppermute | solution.py:421
  62.2 8.2 %interp.1 = (f32[512,128]{1,0:T(8,128)}, f32[128,128]{1,0:T(8,128)}, f32[128,512]{1,0:T(8,128)S(1)}, f32[128,128]{1,0:T(8,128)S(1)}, f32[64,128]{1,0:T(8,128)S(1)}, /*index=5*/s32[1]{0:T(128)}) custom-call(s32[2]{0:T(128)S(1)} %pad_add_fusion.where_ref, f32[128,128]{1,0:T(8,128)S(1)} %get-tuple-element.27.leaf_gram_ref, ...), custom_call_target="tpu_custom_call" | custom-call | flops 8000000000 | bytes 2000000 | tf_op jit(solution)/shard_map/interp/pallas_call | solution.py:350
  70.4 0.0 collective-permute-done.5.across_ref
  70.4 5.9 %top.1 = (f32[64,128]{1,0:T(8,128)}, f32[32,128]{1,0:T(8,128)}) custom-call(s32[2]{0:T(128)S(1)} %pad_add_fusion.where_ref, s32[1]{0:T(128)} %get-tuple-element.33.count_ref, bf16[128,256]{1,0:T(8,128)(2,1)S(1)} %get-tuple-element.30.pick_ref, f32[128,512]{1,0:T(8,128)S(1)} %pair.1.upper_ref, f32[128,512]{1,0:T(8,128)S(1)} %collective-permute-done.5.across_ref, ...), custom_call_target="tpu_custom_call" | custom-call | tf_op jit(solution)/shard_map/top/pallas_call | solution.py:402
  (9 shorter events, 0.1 us)
Async XLA Ops:
  3.5 18.6 %copy-start.5 = (bf16[256,2,128]{2,1,0:T(2,128)(2,1)S(1)}, bf16[256,2,128]{2,1,0:T(2,128)(2,1)}, u32[]{:S(2)}) copy-start(bf16[256,2,128]{2,1,0:T(2,128)(2,1)} %param.10) | copy-start | bytes 393220
  3.5 18.6 %copy-start.6 = (bf16[2,64,128]{2,1,0:T(8,128)(2,1)S(1)}, bf16[2,64,128]{2,1,0:T(8,128)(2,1)}, u32[]{:S(2)}) copy-start(bf16[2,64,128]{2,1,0:T(8,128)(2,1)} %param.14) | copy-start | bytes 98308
  3.5 43.4 %all-to-all-start = ((bf16[640,2,128]{2,1,0:T(2,128)(2,1)}), bf16[640,2,128]{2,1,0:T(2,128)(2,1)S(1)}, u32[]{:S(2)}, u32[]{:S(2)}) async-start(bf16[640,2,128]{2,1,0:T(2,128)(2,1)} %bitcast.16), calls=%async_computation | async-start | bytes 655360 | tf_op jit(solution)/shard_map/all_to_all | solution.py:442
  34.3 18.4 %collective-permute-start.1 = (bf16[4,512,128]{2,1,0:T(8,128)(2,1)S(1)}, bf16[4,512,128]{2,1,0:T(8,128)(2,1)S(1)}, u32[]{:S(2)}, u32[]{:S(2)}) collective-permute-start(bf16[4,512,128]{2,1,0:T(8,128)(2,1)S(1)} %slice.19.x_ref), channel_id=1, source_target_pairs={{8,16},{12,20},{24,32},{28,36},{40,48},{44,52},{56,64},{60,68},{72... | collective-permute-start | bytes 1572872 | tf_op jit(solution)/shard_map/ppermute | solution.py:427
  35.0 17.7 %collective-permute-start = (bf16[4,512,128]{2,1,0:T(8,128)(2,1)S(1)}, bf16[4,512,128]{2,1,0:T(8,128)(2,1)S(1)}, u32[]{:S(2)}, u32[]{:S(2)}) collective-permute-start(bf16[4,512,128]{2,1,0:T(8,128)(2,1)S(1)} %slice.19.x_ref), channel_id=1, source_target_pairs={{0,8},{4,12},{8,0},{12,4},{16,24},{20,28},{24,16},{28,20},{32,40},... | collective-permute-start | bytes 1572872 | tf_op jit(solution)/shard_map/ppermute | solution.py:421
  40.3 12.5 %collective-permute-start.3 = (bf16[4,2,128]{2,1,0:T(2,128)(2,1)S(1)}, bf16[4,2,128]{2,1,0:T(2,128)(2,1)S(1)}, u32[]{:S(2)}, u32[]{:S(2)}) collective-permute-start(bf16[4,2,128]{2,1,0:T(2,128)(2,1)S(1)} %get-tuple-element.39), channel_id=1, source_target_pairs={{4,0},{8,4},{12,8},{16,12},{20,16},{24,20},{28,24},{32,28},{36,32}... | collective-permute-start | bytes 6152 | tf_op jit(solution)/shard_map/ppermute | solution.py:416
  44.9 7.9 %collective-permute-start.2 = (bf16[4,2,128]{2,1,0:T(2,128)(2,1)S(1)}, bf16[4,2,128]{2,1,0:T(2,128)(2,1)S(1)}, u32[]{:S(2)}, u32[]{:S(2)}) collective-permute-start(bf16[4,2,128]{2,1,0:T(2,128)(2,1)S(1)} %get-tuple-element.40), channel_id=1, source_target_pairs={{0,4},{4,8},{8,12},{12,16},{16,20},{20,24},{24,28},{28,32},{32,36}... | collective-permute-start | bytes 6152 | tf_op jit(solution)/shard_map/ppermute | solution.py:416
  46.8 0.8 copy-start
  46.8 0.8 copy-start.3
  46.8 0.7 copy-start.1
  46.9 0.7 copy-start.2
  46.9 0.7 copy-start.4
  54.5 3.5 %collective-permute-start.4 = (f32[128,512]{1,0:T(8,128)S(1)}, f32[128,512]{1,0:T(8,128)S(1)}, u32[]{:S(2)}, u32[]{:S(2)}) collective-permute-start(f32[128,512]{1,0:T(8,128)S(1)} %get-tuple-element.26.chosen_ref.own_ref), channel_id=1, source_target_pairs={{0,4},{4,0},{8,12},{12,8},{16,20},{20,16},{24,28},{28,24},{32,36},... | collective-permute-start | bytes 786440 | tf_op jit(solution)/shard_map/ppermute | solution.py:421
  58.3 12.1 %collective-permute-start.5 = (f32[128,512]{1,0:T(8,128)S(1)}, f32[128,512]{1,0:T(8,128)S(1)}, u32[]{:S(2)}, u32[]{:S(2)}) collective-permute-start(f32[128,512]{1,0:T(8,128)S(1)} %pair.1.upper_ref), channel_id=1, source_target_pairs={{0,8},{4,12},{8,0},{12,4},{16,24},{20,28},{24,16},{28,20},{32,40},... | collective-permute-start | bytes 786440 | tf_op jit(solution)/shard_map/ppermute | solution.py:421

commit v5 on v4

--- a/solution.py
+++ b/solution.py
@@ -178,7 +178,7 @@
     )(where, got, coef, x, *others)
 
 
-def leaf_kernel(where_ref, part_ref, low_ref, high_ref, left_ref, right_ref, pick_ref, own_ref, leaf_ref, chosen_ref):
+def leaf_kernel(where_ref, part_ref, low_ref, high_ref, left_ref, right_ref, pick_ref, leaf_ref, chosen_ref):
     parts, rows, width = part_ref.shape
     sub = iota((8, width), 0)
     for s in range(parts):
@@ -188,7 +188,6 @@
         last = jnp.where(sub == 6, right[0:1], jnp.where(sub == 7, right[1:2], 0.0))
         leaf_ref[s, 0:8, :] = leaf_ref[s, 0:8, :] - first
         leaf_ref[s, rows - 8 : rows, :] = leaf_ref[s, rows - 8 : rows, :] - last
-    own_ref[...] = leaf_ref[where_ref[1]]
     chosen_ref[...] = picked(pick_ref[...], side_by_side(leaf_ref))
 
 
@@ -197,12 +196,11 @@
     return pl.pallas_call(
         leaf_kernel,
         out_shape=[
-            jax.ShapeDtypeStruct((rows, width), F32),
             jax.ShapeDtypeStruct(part.shape, F32),
             jax.ShapeDtypeStruct((RANK, parts * width), F32),
         ],
         in_specs=[pl.BlockSpec(memory_space=pltpu.SMEM)] + [pl.BlockSpec(memory_space=pltpu.VMEM)] * 6,
-        out_specs=[pl.BlockSpec(memory_space=pltpu.VMEM)] * 3,
+        out_specs=[pl.BlockSpec(memory_space=pltpu.VMEM)] * 2,
         compiler_params=pltpu.CompilerParams(vmem_limit_bytes=VMEM_LIMIT),
         name="leaf",
     )(where, part, *others)
@@ -324,9 +322,11 @@
 
 
 def interp_kernel(
-    where_ref, leaf_gram_ref, leaf_cross_ref, chosen_ref, upper_ref, pick_ref,
-    leaf_out, merge_out, mine_out, inverse_out, part_out, count_out,
+    where_ref, leaf_ref, leaf_gram_ref, leaf_cross_ref, chosen_ref, upper_ref, pick_ref,
+    own_out, leaf_out, merge_out, mine_out, inverse_out, part_out, count_out, own_sem,
 ):
+    leave = pltpu.make_async_copy(leaf_ref.at[where_ref[1]], own_out, own_sem)
+    leave.start()
     upper = upper_ref[...]
     pick = pick_ref[:, :RANK]
     mine = picked(pick, upper)
@@ -344,12 +344,14 @@
     part_out[...] = dot(dot(half, mine, ROW_ROW, HIGHEST), mine_inverse - others, precision=HIGHEST)
     leaf_out[...] = dot(leaf_cross_ref[...], leaf_inverse, precision=HIGHEST)
     merge_out[...] = dot(merge_cross, merge_inverse, precision=HIGHEST)
-
-
-def interp(where, leaf_gram, leaf_cross, chosen, upper, pick):
+    leave.wait()
+
+
+def interp(where, leaf_rows, leaf_gram, leaf_cross, chosen, upper, pick):
     return pl.pallas_call(
         interp_kernel,
         out_shape=[
+            jax.ShapeDtypeStruct(leaf_rows.shape[1:], F32),
             jax.ShapeDtypeStruct(leaf_cross.shape, F32),
             jax.ShapeDtypeStruct((RANK, RANK), F32),
             jax.ShapeDtypeStruct(upper.shape, F32),
@@ -357,12 +359,15 @@
             jax.ShapeDtypeStruct((RANK // 2, RANK), F32),
             jax.ShapeDtypeStruct((1,), jnp.int32),
         ],
-        in_specs=[pl.BlockSpec(memory_space=pltpu.SMEM)] + [pl.BlockSpec(memory_space=pltpu.VMEM)] * 5,
-        out_specs=[pl.BlockSpec(memory_space=pltpu.VMEM)] * 5 + [pl.BlockSpec(memory_space=pltpu.SMEM)],
+        in_specs=[pl.BlockSpec(memory_space=pltpu.SMEM)] + [pl.BlockSpec(memory_space=pltpu.VMEM)] * 6,
+        out_specs=[pl.BlockSpec(memory_space=pl.ANY)]
+        + [pl.BlockSpec(memory_space=pltpu.VMEM)] * 5
+        + [pl.BlockSpec(memory_space=pltpu.SMEM)],
+        scratch_shapes=[pltpu.SemaphoreType.DMA],
         cost_estimate=pl.CostEstimate(flops=8_000_000_000, bytes_accessed=2_000_000, transcendentals=0),
         compiler_params=pltpu.CompilerParams(vmem_limit_bytes=VMEM_LIMIT),
         name="interp",
-    )(where, leaf_gram, leaf_cross, chosen, upper, pick)
+    )(where, leaf_rows, leaf_gram, leaf_cross, chosen, upper, pick)
 
 
 def top_kernel(
@@ -450,11 +455,11 @@
         where, got, coef, wide, shift_real.reshape(-1, 128), shift_imag.reshape(-1, 128),
         leaf_skel, pair_skel, quad_skel,
     )
-    own, leaf_rows, chosen = leaf(where, base, low, high, left, right, leaf_pick)
+    leaf_rows, chosen = leaf(where, base, low, high, left, right, leaf_pick)
     leaf_gram, leaf_cross = products(leaf_rows, chosen)
     upper = pair(pair_pick, chosen, swapped(chosen, "row", 0))
-    leaf_interp, merge_interp, mine, inverse, part, count = interp(
-        where, leaf_gram, leaf_cross, chosen, upper, quad_pick
+    own, leaf_interp, merge_interp, mine, inverse, part, count = interp(
+        where, leaf_rows, leaf_gram, leaf_cross, chosen, upper, quad_pick
     )
     top_interp, top_rows = top(where, count, quad_pick, upper, swapped(upper, "row", 1), mine, inverse, part)
     return own.reshape(row_count, 2, col_count), leaf_interp, merge_interp, top_interp, top_rows

time: 76.7 us -> 77 us (level)
  transfers between devices with their start and end apart: 7 -> 7, of which waited for: 1 -> 1; matrix products, arithmetic and copies ran while one was open for 0% -> 0% of each run, Pallas kernels for 17% -> 18%
where the time goes in v5:
time: 77 us; the launch traced here: 76.8 us
  starting transfers between devices  37.1 us (48%)
  Pallas kernels  24.2 us (31%)
  blocking collectives  12.2 us (16%)
  waiting for transfers between devices  1.62 us (2%)
  between operations  0.83 us (1%)
    all_to_all x1, starting transfers between devices, body(): lax.all_to_all(outgoing.reshape(devices * SLOT // 2, 2, -1), 'row', split...  18.5 us
    all_gather x1, blocking collectives, body(): lax.all_gather(jnp.concatenate([probe.reshape(-1, col_count), child_coef....  12.2 us
    ppermute x3, starting transfers between devices, swapped(): lax.ppermute(block, axis, [(i, i ^ 1 << apart) for i in range(count)])  11.4 us
    pallas_call x1, Pallas kernels, interp(): pl.pallas_call(interp_kernel, out_shape=[jax.ShapeDtypeStruct(leaf_rows.s...  8.77 us
    ppermute x2, starting transfers between devices, shifted(): lax.ppermute(value, axis, [(source, source + steps) for source in range(f...  6.49 us
    pallas_call x1, Pallas kernels, top(): pl.pallas_call(top_kernel, out_shape=[jax.ShapeDtypeStruct((RANK // 2, RA...  6.38 us
    pallas_call x1, Pallas kernels, child(): pl.pallas_call(child_kernel, out_shape=[jax.ShapeDtypeStruct((coef.shape[...  3.51 us
    pallas_call x1, Pallas kernels, route(): pl.pallas_call(route_kernel, out_shape=jax.ShapeDtypeStruct((devices * SL...  2.88 us
  transfers between devices with their start and end apart: 7, of which 1 were waited for; matrix products, arithmetic and copies ran while one was open for 0% of the time, Pallas kernels for 18%

profile of v5, /device:TPU:1, one launch (start us, length us, event | category | flops | bytes accessed | tf_op | source)
XLA Modules:
  0.0 76.8 jit_solution(9987095227557483055)
XLA Ops:
  0.6 2.9 %route.1 = bf16[1280,128]{1,0:T(8,128)(2,1)} custom-call(s32[4]{0:T(128)} %of_ref.1, s32[4,128]{1,0:T(4,128)} %map_ref.1, bf16[512,128]{1,0:T(8,128)(2,1)} %gen_ref.1), custom_call_target="tpu_custom_call" | custom-call | tf_op jit(solution)/shard_map/route/pallas_call | solution.py:89
  3.5 18.5 %all-to-all-start = ((bf16[640,2,128]{2,1,0:T(2,128)(2,1)}), bf16[640,2,128]{2,1,0:T(2,128)(2,1)S(1)}, u32[]{:S(2)}, u32[]{:S(2)}) async-start(bf16[640,2,128]{2,1,0:T(2,128)(2,1)} %bitcast.16), calls=%async_computation | async-start | bytes 655360 | tf_op jit(solution)/shard_map/all_to_all | solution.py:447
  22.1 0.0 copy-done.5
  22.1 0.0 copy-done.6
  22.1 12.2 %all-gather = bf16[2560,128]{1,0:T(8,128)(2,1)S(1)} all-gather(bf16[640,128]{1,0:T(8,128)(2,1)S(1)} %pad_maximum_fusion), channel_id=2, replica_groups=mesh['row'=128,'samp'=4] {'samp'}, dimensions={0}, use_global_device_ids=true | all-gather | bytes 819200 | tf_op jit(solution)/shard_map/all_gather | solution.py:442
  34.3 0.7 collective-permute-start.1
  35.0 5.2 %collective-permute-start = (bf16[4,512,128]{2,1,0:T(8,128)(2,1)S(1)}, bf16[4,512,128]{2,1,0:T(8,128)(2,1)S(1)}, u32[]{:S(2)}, u32[]{:S(2)}) collective-permute-start(bf16[4,512,128]{2,1,0:T(8,128)(2,1)S(1)} %slice.19.x_ref), channel_id=1, source_target_pairs={{0,8},{4,12},{8,0},{12,4},{16,24},{20,28},{24,16},{28,20},{32,40},... | collective-permute-start | bytes 1572872 | tf_op jit(solution)/shard_map/ppermute | solution.py:426
  40.3 4.6 %collective-permute-start.3 = (bf16[4,2,128]{2,1,0:T(2,128)(2,1)S(1)}, bf16[4,2,128]{2,1,0:T(2,128)(2,1)S(1)}, u32[]{:S(2)}, u32[]{:S(2)}) collective-permute-start(bf16[4,2,128]{2,1,0:T(2,128)(2,1)S(1)} %get-tuple-element.39), channel_id=1, source_target_pairs={{4,0},{8,4},{12,8},{16,12},{20,16},{24,20},{28,24},{32,28},{36,32}... | collective-permute-start | bytes 6152 | tf_op jit(solution)/shard_map/ppermute | solution.py:421
  44.9 1.9 %collective-permute-start.2 = (bf16[4,2,128]{2,1,0:T(2,128)(2,1)S(1)}, bf16[4,2,128]{2,1,0:T(2,128)(2,1)S(1)}, u32[]{:S(2)}, u32[]{:S(2)}) collective-permute-start(bf16[4,2,128]{2,1,0:T(2,128)(2,1)S(1)} %get-tuple-element.40), channel_id=1, source_target_pairs={{0,4},{4,8},{8,12},{12,16},{16,20},{20,24},{24,28},{28,32},{32,36}... | collective-permute-start | bytes 6152 | tf_op jit(solution)/shard_map/ppermute | solution.py:421
  46.8 0.0 copy-start
  46.8 0.0 copy-start.3
  46.8 0.0 copy-start.1
  46.9 0.1 pad_add_fusion.where_ref
  46.9 0.0 all-to-all-done
  46.9 0.6 copy-done
  47.6 0.0 copy-done.3
  47.6 0.0 copy-done.1
  47.6 0.1 copy-done.2
  47.6 3.5 %child.1 = (f32[4,512,128]{2,1,0:T(8,128)S(1)}, bf16[128,512]{1,0:T(8,128)(2,1)S(1)}, bf16[128,256]{1,0:T(8,128)(2,1)S(1)}, bf16[128,256]{1,0:T(8,128)(2,1)S(1)}) custom-call(s32[2]{0:T(128)S(1)} %pad_add_fusion.where_ref, bf16[1280,128]{1,0:T(8,128)(2,1)S(1)} %bitcast.10, bf16[4,128,128]{2,1,0:T(8,128)(2,1)S(1)} %slice.18.coef_ref, ...), custom_call_target="tpu_custom_call" | custom-call | flops 2000000000 | bytes 2000000 | tf_op jit(solution)/shard_map/child/pallas_call | solution.py:163
  51.1 1.6 %collective-permute-done.3.right_ref = bf16[4,2,128]{2,1,0:T(2,128)(2,1)S(1)} collective-permute-done((bf16[4,2,128]{2,1,0:T(2,128)(2,1)S(1)}, bf16[4,2,128]{2,1,0:T(2,128)(2,1)S(1)}, u32[]{:S(2)}, u32[]{:S(2)}) %collective-permute-start.3) | collective-permute-done | bytes 2080 | tf_op jit(solution)/shard_map/ppermute | solution.py:421
  52.7 0.0 collective-permute-done.2.left_ref
  52.7 0.0 collective-permute-done.1.high_ref
  52.7 0.0 collective-permute-done.low_ref
  52.7 1.1 %leaf.1 = (f32[4,512,128]{2,1,0:T(8,128)S(1)}, f32[128,512]{1,0:T(8,128)S(1)}) custom-call(s32[2]{0:T(128)S(1)} %pad_add_fusion.where_ref, f32[4,512,128]{2,1,0:T(8,128)S(1)} %get-tuple-element.22.part_ref, bf16[4,512,128]{2,1,0:T(8,128)(2,1)S(1)} %collective-permute-done.low_ref, bf16[4,512,128]{2,1,0:T(8,128)(2,1)S(1)} %collective-permute-done.1.high_ref, ...), custom_call_target="tpu_custom_call" | custom-call | tf_op jit(solution)/shard_map/leaf/pallas_call | solution.py:196
  53.9 2.3 %collective-permute-start.4 = (f32[128,512]{1,0:T(8,128)S(1)}, f32[128,512]{1,0:T(8,128)S(1)}, u32[]{:S(2)}, u32[]{:S(2)}) collective-permute-start(f32[128,512]{1,0:T(8,128)S(1)} %get-tuple-element.25.chosen_ref.own_ref), channel_id=1, source_target_pairs={{0,4},{4,0},{8,12},{12,8},{16,20},{20,16},{24,28},{28,24},{32,36},... | collective-permute-start | bytes 786440 | tf_op jit(solution)/shard_map/ppermute | solution.py:426
  56.2 1.2 %products.1 = (f32[128,128]{1,0:T(8,128)S(1)}, f32[512,128]{1,0:T(8,128)S(1)}) custom-call(f32[4,512,128]{2,1,0:T(8,128)S(1)} %get-tuple-element.24.leaf_ref, f32[128,512]{1,0:T(8,128)S(1)} %get-tuple-element.25.chosen_ref.own_ref), custom_call_target="tpu_custom_call" | custom-call | flops 1000000000 | bytes 2000000 | tf_op jit(solution)/shard_map/products/pallas_call | solution.py:216
  57.4 0.0 collective-permute-done.4.other_ref
  57.4 0.3 pair.1.upper_ref
  57.7 3.9 %collective-permute-start.5 = (f32[128,512]{1,0:T(8,128)S(1)}, f32[128,512]{1,0:T(8,128)S(1)}, u32[]{:S(2)}, u32[]{:S(2)}) collective-permute-start(f32[128,512]{1,0:T(8,128)S(1)} %pair.1.upper_ref), channel_id=1, source_target_pairs={{0,8},{4,12},{8,0},{12,4},{16,24},{20,28},{24,16},{28,20},{32,40},... | collective-permute-start | bytes 786440 | tf_op jit(solution)/shard_map/ppermute | solution.py:426
  61.6 8.8 %interp.1 = (f32[512,128]{1,0:T(8,128)}, f32[512,128]{1,0:T(8,128)}, f32[128,128]{1,0:T(8,128)}, f32[128,512]{1,0:T(8,128)S(1)}, f32[128,128]{1,0:T(8,128)S(1)}, /*index=5*/f32[64,128]{1,0:T(8,128)S(1)}, s32[1]{0:T(128)}) custom-call(s32[2]{0:T(128)S(1)} %pad_add_fusion.where_ref, f32[4,512,128]{2,1,0:T(8,128)S(1)} %get-tuple-element.24.leaf_ref, ...), custom_call_target="tpu_custom_call" | custom-call | flops 8000000000 | bytes 2000000 | tf_op jit(solution)/shard_map/interp/pallas_call | solution.py:351
  70.4 0.0 collective-permute-done.5.across_ref
  70.4 6.4 %top.1 = (f32[64,128]{1,0:T(8,128)}, f32[32,128]{1,0:T(8,128)}) custom-call(s32[2]{0:T(128)S(1)} %pad_add_fusion.where_ref, s32[1]{0:T(128)} %get-tuple-element.33.count_ref, bf16[128,256]{1,0:T(8,128)(2,1)S(1)} %get-tuple-element.29.pick_ref, f32[128,512]{1,0:T(8,128)S(1)} %pair.1.upper_ref, f32[128,512]{1,0:T(8,128)S(1)} %collective-permute-done.5.across_ref, ...), custom_call_target="tpu_custom_call" | custom-call | tf_op jit(solution)/shard_map/top/pallas_call | solution.py:407
  (9 shorter events, 0.1 us)
Async XLA Ops:
  3.5 18.6 %copy-start.5 = (bf16[256,2,128]{2,1,0:T(2,128)(2,1)S(1)}, bf16[256,2,128]{2,1,0:T(2,128)(2,1)}, u32[]{:S(2)}) copy-start(bf16[256,2,128]{2,1,0:T(2,128)(2,1)} %param.10) | copy-start | bytes 393220
  3.5 18.6 %copy-start.6 = (bf16[2,64,128]{2,1,0:T(8,128)(2,1)S(1)}, bf16[2,64,128]{2,1,0:T(8,128)(2,1)}, u32[]{:S(2)}) copy-start(bf16[2,64,128]{2,1,0:T(8,128)(2,1)} %param.14) | copy-start | bytes 98308
  3.5 43.4 %all-to-all-start = ((bf16[640,2,128]{2,1,0:T(2,128)(2,1)}), bf16[640,2,128]{2,1,0:T(2,128)(2,1)S(1)}, u32[]{:S(2)}, u32[]{:S(2)}) async-start(bf16[640,2,128]{2,1,0:T(2,128)(2,1)} %bitcast.16), calls=%async_computation | async-start | bytes 655360 | tf_op jit(solution)/shard_map/all_to_all | solution.py:447
  34.3 18.4 %collective-permute-start.1 = (bf16[4,512,128]{2,1,0:T(8,128)(2,1)S(1)}, bf16[4,512,128]{2,1,0:T(8,128)(2,1)S(1)}, u32[]{:S(2)}, u32[]{:S(2)}) collective-permute-start(bf16[4,512,128]{2,1,0:T(8,128)(2,1)S(1)} %slice.19.x_ref), channel_id=1, source_target_pairs={{8,16},{12,20},{24,32},{28,36},{40,48},{44,52},{56,64},{60,68},{72... | collective-permute-start | bytes 1572872 | tf_op jit(solution)/shard_map/ppermute | solution.py:432
  35.0 17.7 %collective-permute-start = (bf16[4,512,128]{2,1,0:T(8,128)(2,1)S(1)}, bf16[4,512,128]{2,1,0:T(8,128)(2,1)S(1)}, u32[]{:S(2)}, u32[]{:S(2)}) collective-permute-start(bf16[4,512,128]{2,1,0:T(8,128)(2,1)S(1)} %slice.19.x_ref), channel_id=1, source_target_pairs={{0,8},{4,12},{8,0},{12,4},{16,24},{20,28},{24,16},{28,20},{32,40},... | collective-permute-start | bytes 1572872 | tf_op jit(solution)/shard_map/ppermute | solution.py:426
  40.3 12.5 %collective-permute-start.3 = (bf16[4,2,128]{2,1,0:T(2,128)(2,1)S(1)}, bf16[4,2,128]{2,1,0:T(2,128)(2,1)S(1)}, u32[]{:S(2)}, u32[]{:S(2)}) collective-permute-start(bf16[4,2,128]{2,1,0:T(2,128)(2,1)S(1)} %get-tuple-element.39), channel_id=1, source_target_pairs={{4,0},{8,4},{12,8},{16,12},{20,16},{24,20},{28,24},{32,28},{36,32}... | collective-permute-start | bytes 6152 | tf_op jit(solution)/shard_map/ppermute | solution.py:421
  44.9 7.9 %collective-permute-start.2 = (bf16[4,2,128]{2,1,0:T(2,128)(2,1)S(1)}, bf16[4,2,128]{2,1,0:T(2,128)(2,1)S(1)}, u32[]{:S(2)}, u32[]{:S(2)}) collective-permute-start(bf16[4,2,128]{2,1,0:T(2,128)(2,1)S(1)} %get-tuple-element.40), channel_id=1, source_target_pairs={{0,4},{4,8},{8,12},{12,16},{16,20},{20,24},{24,28},{28,32},{32,36}... | collective-permute-start | bytes 6152 | tf_op jit(solution)/shard_map/ppermute | solution.py:421
  46.8 0.8 copy-start
  46.8 0.8 copy-start.3
  46.8 0.7 copy-start.1
  46.9 0.7 copy-start.2
  46.9 0.7 copy-start.4
  53.9 3.5 %collective-permute-start.4 = (f32[128,512]{1,0:T(8,128)S(1)}, f32[128,512]{1,0:T(8,128)S(1)}, u32[]{:S(2)}, u32[]{:S(2)}) collective-permute-start(f32[128,512]{1,0:T(8,128)S(1)} %get-tuple-element.25.chosen_ref.own_ref), channel_id=1, source_target_pairs={{0,4},{4,0},{8,12},{12,8},{16,20},{20,16},{24,28},{28,24},{32,36},... | collective-permute-start | bytes 786440 | tf_op jit(solution)/shard_map/ppermute | solution.py:426
  57.7 12.7 %collective-permute-start.5 = (f32[128,512]{1,0:T(8,128)S(1)}, f32[128,512]{1,0:T(8,128)S(1)}, u32[]{:S(2)}, u32[]{:S(2)}) collective-permute-start(f32[128,512]{1,0:T(8,128)S(1)} %pair.1.upper_ref), channel_id=1, source_target_pairs={{0,8},{4,12},{8,0},{12,4},{16,24},{20,28},{24,16},{28,20},{32,40},... | collective-permute-start | bytes 786440 | tf_op jit(solution)/shard_map/ppermute | solution.py:426
